TPU v7x, 32 devices: a whole 2x2x4 slice. The times are simulated.
32 devices in a mesh: blk: 8 (over z, x), feat: 4 (over y, core).
Axes of the slice: x: 2, y: 2, z: 4, core: 2. Of those that a mesh axis runs over, the one named last changes fastest.
Arguments:
- conv_maps: bfloat16 [1024, 169, 512], P('blk', None, 'feat'), may hold values from -18 to 18
- crop_counts: int32 [256], P('blk'), may hold values from 1 to 4, as said below
- fc_weight: bfloat16 [2, 4096, 9216], P(None, 'blk', 'feat'), may hold values from -0.0625 to 0.0625
- fc_bias: float32 [2, 4096], replicated, may hold values from -3 to 3
- stitch_in: float32 [2, 2, 256], P(None, None, 'feat'), may hold values from 0.3 to 1.2
- stitch_out: float32 [2, 2, 4096], P(None, None, 'feat'), may hold values from 0.3 to 1.2
- cotangent: bfloat16 [1024, 2, 4096], P('blk', None, 'feat'), may hold values from -6 to 6
Outputs:
- activations: bfloat16 [1024, 2, 4096], P('blk', None, 'feat')
- conv_grad: bfloat16 [1024, 169, 512], P('blk', None, 'feat')
- weight_grad: float32 [2, 4096, 9216], P(None, 'blk', 'feat')
- bias_grad: float32 [2, 4096], P(None, 'blk')
- stitch_in_grad: float32 [2, 2, 256], P(None, None, 'feat')
- stitch_out_grad: float32 [2, 2, 4096], P(None, None, 'feat')
Inputs may be any that keep to these rules, and one draw needn't show every extreme that they name: `crop_counts`: each image has 1 to 4 crops; a blk index's slots hold its images' crops first, the rest of its 128 slots are padding; in every draw some blk index has all its images at 4 crops.
All inputs are finite; a program needn't handle non-finite values.
Results may differ from a plain program's by a relative error of at most 0.0054.
Values may be sent and summed in bfloat16 or wider, within the bound.
A program may use at most 256 MiB of HBM per device.

v0:
```python
import jax
import jax.numpy as jnp
from jax import lax
from jax.sharding import PartitionSpec as P

MAP = 13
GRID = 6
TOWERS = 2


def pool_table(dtype):
    position = jnp.arange(MAP * MAP)
    row_pos = position // MAP
    col_pos = position % MAP
    cell = jnp.arange(GRID * GRID)
    row_cell = cell // GRID
    col_cell = cell % GRID
    down = row_pos[:, None] - 2 * row_cell[None, :]
    across = col_pos[:, None] - 2 * col_cell[None, :]
    inside = (down >= 0) & (down < 3) & (across >= 0) & (across < 3)
    return inside.astype(dtype)


def stitch_first(pooled, stitch_in):
    return jnp.einsum("tuc,rucq->rtcq", stitch_in, pooled, precision=lax.Precision.HIGHEST)


def stitch_head(pre, stitch_out):
    act = jax.nn.gelu(pre)
    return jnp.einsum("tuk,ruk->rtk", stitch_out, act, precision=lax.Precision.HIGHEST)


def body(conv_maps, crop_counts, fc_weight, fc_bias, stitch_in, stitch_out, cotangent):
    f32 = jnp.float32
    bf16 = jnp.bfloat16
    num_rows = conv_maps.shape[0]
    merged = conv_maps.shape[2]
    chans = merged // TOWERS
    cols = fc_weight.shape[1]
    feat_idx = lax.axis_index("feat")
    blk_idx = lax.axis_index("blk")
    sums = jnp.einsum("rpm,pq->rqm", conv_maps, pool_table(bf16), preferred_element_type=f32)
    pooled = jnp.transpose(sums.reshape(num_rows, GRID * GRID, chans, TOWERS), (0, 3, 2, 1)) * (
        1.0 / 9.0
    )
    mixed, pull_first = jax.vjp(stitch_first, pooled, stitch_in)
    feats = mixed.astype(bf16).reshape(num_rows, TOWERS, -1)
    own_cols = jnp.einsum(
        "rtf,tnf->rtn",
        lax.all_gather(feats, "blk", axis=0, tiled=True),
        fc_weight,
        preferred_element_type=f32,
    )
    partial_value = lax.all_to_all(own_cols, "blk", split_axis=0, concat_axis=2, tiled=True)
    pre = lax.psum_scatter(partial_value, "feat", scatter_dimension=2, tiled=True)
    quarter = pre.shape[2]
    bias_part = lax.dynamic_slice_in_dim(fc_bias, feat_idx * quarter, quarter, 1)
    pre = pre + bias_part[None]
    live = (jnp.arange(num_rows) < jnp.sum(crop_counts)).astype(f32)
    stitched, pull_head = jax.vjp(stitch_head, pre, stitch_out)
    activations = (live[:, None, None] * stitched).astype(bf16)
    grad_out = live[:, None, None] * cotangent.astype(f32)
    grad_pre, grad_so = pull_head(grad_out)
    grad_low = grad_pre.astype(bf16)
    grad_all = lax.all_gather(grad_low, "feat", axis=2, tiled=True)
    bias_terms = jnp.sum(grad_all, axis=0, dtype=f32)
    grad_cols = lax.all_to_all(grad_all, "blk", split_axis=2, concat_axis=0, tiled=True)
    part = grad_cols
    weight_grad = jnp.einsum(
        "rtf,rtn->tnf",
        lax.all_gather(feats, "blk", axis=0, tiled=True),
        part,
        preferred_element_type=f32,
    )
    part = grad_all
    grad_feats = jnp.einsum(
        "rtn,tnf->rtf",
        part,
        lax.all_gather(fc_weight, "blk", axis=1, tiled=True),
        preferred_element_type=f32,
    )
    grad_mixed = grad_feats.reshape(num_rows, TOWERS, chans, -1)
    grad_pooled, grad_si = pull_first(grad_mixed)
    spread = jnp.einsum(
        "rtcq,pq->rpct", grad_pooled * (1.0 / 9.0), pool_table(f32), precision=lax.Precision.HIGHEST
    )
    conv_grad = spread.reshape(num_rows, MAP * MAP, merged).astype(bf16)
    stitch_in_grad, stitch_out_grad, bias_total = lax.psum((grad_si, grad_so, bias_terms), "blk")
    bias_grad = lax.dynamic_slice_in_dim(bias_total, blk_idx * cols, cols, 1)
    return (activations, conv_grad, weight_grad, bias_grad, stitch_in_grad, stitch_out_grad)


def solution(mesh):
    return jax.shard_map(
        body,
        mesh=mesh,
        in_specs=(
            P("blk", None, "feat"),
            P("blk"),
            P(None, "blk", "feat"),
            P(),
            P(None, None, "feat"),
            P(None, None, "feat"),
            P("blk", None, "feat"),
        ),
        out_specs=(
            P("blk", None, "feat"),
            P("blk", None, "feat"),
            P(None, "blk", "feat"),
            P(None, "blk"),
            P(None, None, "feat"),
            P(None, None, "feat"),
        ),
        check_vma=False,
    )
```

profile of v0, /device:TPU:0, one launch (start us, length us, event | category | flops | bytes accessed | tf_op | source)
XLA Modules:
  0.0 1357.1 jit_solution(17951694073466181086)
XLA Ops:
  7.3 0.8 copy.102
  8.1 6.1 multiply_bitcast_fusion
  14.1 2.1 copy.74
  16.2 9.8 fusion.10
  26.0 2.7 copy.77
  29.0 140.6 %all-gather.4.cloned.1.call-done = bf16[1024,2,2304]{2,0,1:T(8,128)(2,1)} async-done(((bf16[128,2,2304]{2,0,1:T(8,128)(2,1)}), bf16[1024,2,2304]{2,0,1:T(8,128)(2,1)}) %all-gather.4.cloned.1.call-update) | async-done | bytes 9437200 | tf_op jit(solution)/shard_map/all_gather | solution.py:50
  169.6 9.1 convolution_bitcast_fusion.1
  178.7 3.2 copy.78
  182.0 96.3 %all_to_all.36 = f32[1024,2,512]{2,1,0:T(2,128)} all-to-all(f32[1024,2,512]{2,1,0:T(2,128)S(1)} %copy.78), channel_id=1, replica_groups=mesh['blk'=8,'feat'=4] {'blk'}, dimensions={0} | all-to-all | bytes 8388608 | tf_op jit(solution)/shard_map/all_to_all | solution.py:54
  278.3 9.1 copy.79
  287.5 0.6 copy-done.11
  288.1 0.6 reduce_sum.18
  288.7 0.6 compare_convert_fusion
  289.8 1.3 copy.83
  291.1 0.6 copy.84
  292.1 7.3 fusion.43
  299.3 0.5 copy.85
  299.9 0.6 dynamic-slice
  301.2 70.9 %all-reduce.4.cloned.1.call-done = f32[128,2,4096]{0,1,2:T(2,128)} async-done(((f32[128,2,4096]{0,1,2:T(2,128)}), f32[128,2,4096]{0,1,2:T(2,128)}) %all-reduce.4.cloned.1.call-update) | async-done | bytes 4194320
  372.1 1.3 constant_dynamic-slice_fusion
  373.4 0.5 copy.80
  373.9 1.6 fusion.24
  375.5 2.0 copy.86
  377.5 0.5 all-gather.8.cloned.1.call-update
  378.1 22.3 %all-gather.6.cloned.1.call-done = bf16[128,2,4096]{0,1,2:T(2,128)(2,1)} async-done(((bf16[128,2,1024]{0,1,2:T(2,128)(2,1)}), bf16[128,2,4096]{0,1,2:T(2,128)(2,1)}) %all-gather.6.cloned.1.call-update) | async-done | bytes 2097168 | tf_op jit(solution)/shard_map/all_gather | solution.py:65
  400.4 16.3 %all-to-all-start.1 = ((bf16[128,2,4096]{0,1,2:T(2,128)(2,1)}), bf16[128,2,4096]{0,1,2:T(2,128)(2,1)}, u32[]{:S(2)}, u32[]{:S(2)}) async-start(bf16[128,2,4096]{0,1,2:T(2,128)(2,1)} %all-gather.6.cloned.1.call-done), calls=%async_computation.1 | async-start | bytes 4194304 | tf_op jit(solution)/shard_map/all_to_all | solution.py:67
  416.7 0.6 copy.81
  417.3 9.3 fusion.14
  426.6 3.1 copy.96
  429.7 8.3 convolution_bitcast_fusion.2
  438.0 8.2 convert_reduce_fusion
  446.2 41.7 %all-to-all-done.1 = bf16[128,2,4096]{0,1,2:T(2,128)(2,1)} async-done(((bf16[128,2,4096]{0,1,2:T(2,128)(2,1)}), bf16[128,2,4096]{0,1,2:T(2,128)(2,1)}, u32[]{:S(2)}, u32[]{:S(2)}) %all-to-all-start.1) | async-done | bytes 2097184 | tf_op jit(solution)/shard_map/all_to_all | solution.py:67
  487.8 4.3 copy.126
  492.1 4.2 all_to_all.33
  496.3 11.6 fusion.44
  507.9 632.8 %all-gather.8.cloned.1.call-done = bf16[2,4096,2304]{2,1,0:T(8,128)(2,1)} async-done(((bf16[2,512,2304]{2,1,0:T(8,128)(2,1)}), bf16[2,4096,2304]{2,1,0:T(8,128)(2,1)}) %all-gather.8.cloned.1.call-update) | async-done | bytes 37748752 | tf_op jit(solution)/shard_map/all_gather | solution.py:79
  1140.7 16.1 %convolution_bitcast_fusion = f32[128,2,2304]{2,0,1:T(8,128)} fusion(bf16[2,4096,2304]{2,1,0:T(8,128)(2,1)} %all-gather.8.cloned.1.call-done, bf16[128,2,4096]{0,1,2:T(2,128)(2,1)S(1)} %copy-done.2), kind=kOutput, calls=%fused_computation.4 | convolution fusion | flops 4831838208 | bytes 42205184 | tf_op jit(solution)/shard_map/rtn,tnf->rtf/dot_general | solution.py:76
  1156.9 4.2 copy.88
  1161.1 8.7 multiply_bitcast_fusion.1
  1169.8 20.9 %fusion.15 = f32[2,2,64]{1,0,2:T(2,128)S(1)} fusion(f32[64,128,36,2]{1,3,2,0:T(2,128)S(1)} %bitcast.86, f32[128,2,64,36]{0,1,2,3:T(2,128)S(1)} %bitcast.89), kind=kOutput, calls=%fused_computation.22 | convolution fusion | flops 14155776 | bytes 4719616 | tf_op jit(solution)/shard_map/transpose(jvp(tuc,rucq->rtcq))/dot_general | solution.py:25
  1190.8 5.4 convert_bitcast_fusion
  1196.2 13.0 copy.91
  1209.2 8.3 copy.97
  1217.5 128.3 %all-reduce.1 = (f32[2,4096]{0,1:T(8,128)}, f32[2,2,64]{1,0,2:T(2,128)S(1)}, f32[2,2,1024]{1,0,2:T(2,128)}) all-reduce(f32[2,4096]{0,1:T(8,128)S(1)} %copy-done.3, f32[2,2,64]{1,0,2:T(2,128)S(1)} %fusion.15, f32[2,2,1024]{1,0,2:T(2,128)S(1)} %convolution_bitcast_fusion.2), channel_id=1, replica_groups=mesh['blk'=8,'feat'=4] {'blk'}, use_global_device_ids=true, to_apply=%region_3.4 | all-reduce | flops 12544 | bytes 100352 | tf_op jit(solution)/shard_map/psum | solution.py:88
  1345.8 1.0 constant_dynamic-slice_fusion.1
  1346.8 0.7 copy.98
  1347.5 0.7 copy.99
  1348.2 2.0 copy.100
  (36 shorter events, 1.4 us)
Async XLA Ops:
  7.2 294.0 %copy-start = (f32[2,4096]{1,0:T(2,128)S(1)}, f32[2,4096]{1,0:T(2,128)}, u32[]{:S(2)}) copy-start(f32[2,4096]{1,0:T(2,128)} %param.10) | copy-start | bytes 98308
  7.2 162.5 %all-gather.4.cloned.1.call-start = ((), (), s32[]{:S(2)}) async-start(), calls=%async_computation.2 | async-start | bytes 10616832 | tf_op jit(solution)/shard_map/all_gather | solution.py:50
  28.7 343.3 %all-reduce.4.cloned.1.call-start = ((), (), s32[]{:S(2)}) async-start(), calls=%async_computation.5 | async-start | bytes 8388608
  287.4 0.7 copy-start.11
  287.4 1.9 copy-start.9
  287.4 3.6 copy-start.10
  287.5 112.9 %all-gather.6.cloned.1.call-start = ((), (), s32[]{:S(2)}) async-start(), calls=%async_computation.3 | async-start | bytes 2621440 | tf_op jit(solution)/shard_map/all_gather | solution.py:65
  291.1 1.0 copy-start.5
  292.1 7.8 copy-start.6
  292.1 7.8 copy-start.12
  377.5 763.2 %all-gather.8.cloned.1.call-start = ((), (), s32[]{:S(2)}) async-start(), calls=%async_computation.4 | async-start | bytes 42467328 | tf_op jit(solution)/shard_map/all_gather | solution.py:79
  378.1 39.2 %copy-start.7 = (f32[2,2,1024]{0,1,2:T(2,128)S(1)}, f32[2,2,1024]{0,1,2:T(2,128)}, u32[]{:S(2)}) copy-start(f32[2,2,1024]{0,1,2:T(2,128)} %copy-done.6) | copy-start | bytes 49156
  400.4 87.5 %all-to-all-start.1 = ((bf16[128,2,4096]{0,1,2:T(2,128)(2,1)}), bf16[128,2,4096]{0,1,2:T(2,128)(2,1)}, u32[]{:S(2)}, u32[]{:S(2)}) async-start(bf16[128,2,4096]{0,1,2:T(2,128)(2,1)} %all-gather.6.cloned.1.call-done), calls=%async_computation.1 | async-start | bytes 4194304 | tf_op jit(solution)/shard_map/all_to_all | solution.py:67
  417.3 9.3 copy-start.8
  426.6 11.4 copy-start.2
  1161.1 8.7 copy-start.4
  1209.2 8.3 copy-start.3
  1209.2 141.0 %copy-start.1 = (f32[2,4096]{1,0:T(2,128)S(1)}, f32[2,4096]{1,0:T(2,128)}, u32[]{:S(2)}) copy-start(f32[2,4096]{1,0:T(2,128)} %param.10) | copy-start | bytes 98308
Sparse Core Ops, SparseCore 0:
  28.8 140.7 all-gather.3
  287.6 84.4 all-reduce.3
  377.6 22.7 all-gather.5
  401.8 738.8 all-gather.7
where the time goes:
time: 1360 us
  waiting for transfers between devices  909 us (67%)
  blocking collectives  225 us (17%)
  matrix products  113 us (8%)
  local copies, waits for them, and re-layouts  67.8 us (5%)
  starting transfers between devices  16.7 us (1%)
  between operations  15.2 us (1%)
    all_gather x1, waiting for transfers between devices, body(): lax.all_gather(fc_weight, 'blk', axis=1, tiled=True)  633 us
    all_gather x1, waiting for transfers between devices, body(): lax.all_gather(feats, 'blk', axis=0, tiled=True)  141 us
    psum x1, blocking collectives, body(): lax.psum((grad_si, grad_so, bias_terms), 'blk')  128 us
    all_to_all x1, blocking collectives, body(): lax.all_to_all(own_cols, 'blk', split_axis=0, concat_axis=2, tiled=True)  96.3 us
    unnamed x5, waiting for transfers between devices  71.5 us
    all_to_all x1, waiting for transfers between devices, body(): lax.all_to_all(grad_all, 'blk', split_axis=2, concat_axis=0, tiled=True)  41.7 us
    dot_general x3, matrix products, stitch_first(): jnp.einsum('tuc,rucq->rtcq', stitch_in, pooled, precision=lax.Precision.H...  39.4 us
  transfers between devices with their start and end apart: 5, of which 5 were waited for; matrix products, arithmetic and copies ran while one was open for 4% of the time, Pallas kernels for 0%

commit v1 on v0

--- a/solution.py
+++ b/solution.py
@@ -1,11 +1,24 @@
+import functools
+
 import jax
 import jax.numpy as jnp
 from jax import lax
+from jax.experimental import pallas as pl
+from jax.experimental.pallas import tpu as pltpu
 from jax.sharding import PartitionSpec as P
 
 MAP = 13
 GRID = 6
 TOWERS = 2
+CHUNK = 16
+SPAN = 4
+PLACES = 8
+FEATS = 4
+RING_BLK = (0, 2, 4, 6, 7, 5, 3, 1)
+MESH = pl.DeviceIdType.MESH
+f32 = jnp.float32
+bf16 = jnp.bfloat16
+i32 = jnp.int32
 
 
 def pool_table(dtype):
@@ -30,9 +43,7 @@
     return jnp.einsum("tuk,ruk->rtk", stitch_out, act, precision=lax.Precision.HIGHEST)
 
 
-def body(conv_maps, crop_counts, fc_weight, fc_bias, stitch_in, stitch_out, cotangent):
-    f32 = jnp.float32
-    bf16 = jnp.bfloat16
+def body_plain(conv_maps, crop_counts, fc_weight, fc_bias, stitch_in, stitch_out, cotangent):
     num_rows = conv_maps.shape[0]
     merged = conv_maps.shape[2]
     chans = merged // TOWERS
@@ -65,17 +76,15 @@
     grad_all = lax.all_gather(grad_low, "feat", axis=2, tiled=True)
     bias_terms = jnp.sum(grad_all, axis=0, dtype=f32)
     grad_cols = lax.all_to_all(grad_all, "blk", split_axis=2, concat_axis=0, tiled=True)
-    part = grad_cols
     weight_grad = jnp.einsum(
         "rtf,rtn->tnf",
         lax.all_gather(feats, "blk", axis=0, tiled=True),
-        part,
+        grad_cols,
         preferred_element_type=f32,
     )
-    part = grad_all
     grad_feats = jnp.einsum(
         "rtn,tnf->rtf",
-        part,
+        grad_all,
         lax.all_gather(fc_weight, "blk", axis=1, tiled=True),
         preferred_element_type=f32,
     )
@@ -90,9 +99,610 @@
     return (activations, conv_grad, weight_grad, bias_grad, stitch_in_grad, stitch_out_grad)
 
 
+def ring_place(blk):
+    z, x = lax.div(blk, 2), lax.rem(blk, 2)
+    return z + x * (7 - 2 * z)
+
+
+def ring_blk(place):
+    x = lax.div(place, 4)
+    return 2 * (place + x * (7 - 2 * place)) + x
+
+
+def fc_kernel(
+    steps,
+    n_ref, so_ref, bias_ref, x_ref, cot_ref, w_hbm,
+    act_out, gf_out, wg_hbm, bg_out, sog_out,
+    w, x, land, ring_tx, ex_tx, ex_rx, gp, part, sum_rx, held, sums,
+    cot_rx, acts, act_tx, act_rx, sog_acc, sog_tx, sog_rx, wg_tx,
+    kd, nn, start, tot, slot_rc, slot_live,
+    w_sem, ag_ss, ag_rs, rs_ss, rs_rs, ex_ss, ex_rs, gp_ss, gp_rs,
+    cot_ss, cot_rs, act_ss, act_rs, sog_ss, sog_rs, wg_sem,
+):
+    blk, feat = lax.axis_index("blk"), lax.axis_index("feat")
+    place = ring_place(blk)
+    ring_to = (ring_blk(lax.rem(place + 1, 8)), ring_blk(lax.rem(place + 7, 8)))
+    ring_from = (lax.rem(place + 7, 8), lax.rem(place + 1, 8))
+    groups = x.shape[0] - 1
+    slots = groups * SPAN
+    sent = 2 * (steps - 1)
+    feats_dim = x.shape[-1]
+    units = w.shape[1]
+    quarter = units // FEATS
+    row_feat = lax.div(blk, 2)
+    half_at = lax.rem(blk, 2) * FEATS + feat
+    mine = row_feat == feat
+
+    w_copy = pltpu.make_async_copy(w_hbm, w, w_sem)
+    w_copy.start()
+
+    bar = pltpu.get_barrier_semaphore()
+
+    def hello(dev):
+        pl.semaphore_signal(bar, inc=1, device_id=dev, device_id_type=MESH)
+
+    for d in (0, 1):
+        hello((ring_to[d], feat))
+    for o in range(1, FEATS):
+        hello((blk, lax.rem(feat + o, FEATS)))
+
+    def hello_far(s, carry):
+        to = (2 * feat + lax.div(s, FEATS), lax.rem(s, FEATS))
+
+        @pl.when(jnp.logical_or(to[0] != blk, to[1] != feat))
+        def _():
+            hello(to)
+
+        @pl.when(jnp.logical_or(s != blk, row_feat != feat))
+        def _():
+            hello((s, row_feat))
+
+        return carry
+
+    lax.fori_loop(0, 8, hello_far, 0)
+    pl.semaphore_wait(bar, jnp.where(mine, 2 + 3 + 14, 2 + 3 + 16))
+
+    def cot_copy(s):
+        return pltpu.make_async_remote_copy(
+            src_ref=cot_ref.at[s], dst_ref=cot_rx.at[blk], send_sem=cot_ss.at[s],
+            recv_sem=cot_rs.at[blk],
+            device_id=(2 * feat + lax.div(s, FEATS), lax.rem(s, FEATS)), device_id_type=MESH)
+
+    def cot_wait(r):
+        return pltpu.make_async_remote_copy(
+            src_ref=cot_ref.at[0], dst_ref=cot_rx.at[r], send_sem=cot_ss.at[0],
+            recv_sem=cot_rs.at[r], device_id=(r, row_feat), device_id_type=MESH)
+
+    def far_not_me(s):
+        return jnp.logical_or(2 * feat + lax.div(s, FEATS) != blk, lax.rem(s, FEATS) != feat)
+
+    def near_not_me(r):
+        return jnp.logical_or(r != blk, row_feat != feat)
+
+    for c in range(8):
+        for t in range(TOWERS):
+            x[groups, t, c // SPAN, c % SPAN] = x_ref[c, t]
+
+    run = jnp.int32(0)
+    for q in range(PLACES):
+        n = n_ref[RING_BLK[q]]
+        k = jnp.clip(lax.div(n + (CHUNK - 1), CHUNK), 2, 8)
+        first = lax.div(run + k + 1, 2) - lax.div(run + 1, 2)
+        kd[q] = first
+        kd[PLACES + q] = k - first
+        nn[q] = n
+        run = run + k
+
+    def ring_unit_copy(d, m):
+        return pltpu.make_async_remote_copy(
+            src_ref=ring_tx.at[d, lax.rem(m, 4)], dst_ref=land.at[d, m],
+            send_sem=ag_ss.at[d, lax.rem(m, 4)], recv_sem=ag_rs.at[d, m],
+            device_id=(ring_to[d], feat), device_id_type=MESH)
+
+    own_k = (kd[place], kd[PLACES + place])
+    prev_k = tuple(kd[d * PLACES + ring_from[d]] for d in (0, 1))
+    own_base = (0, own_k[0])
+    for m in (0, 1):
+        for d in (0, 1):
+            c = own_base[d]
+            ring_tx[d, m] = x[groups, m, lax.div(c, SPAN), lax.rem(c, SPAN)] if d else x[groups, m, 0, 0]
+            ring_unit_copy(d, jnp.int32(m)).start()
+
+    def cot_send(s, carry):
+        @pl.when(far_not_me(s))
+        def _():
+            cot_copy(s).start()
+
+        @pl.when(jnp.logical_not(far_not_me(s)))
+        def _():
+            cot_rx[blk] = cot_ref[s]
+
+        return carry
+
+    lax.fori_loop(0, 8, cot_send, 0)
+
+    for d in (0, 1):
+        run = jnp.int32(0)
+        for h in range(1, PLACES + 1):
+            at = lax.rem(place + (PLACES - h if d == 0 else h), PLACES)
+            start[d * PLACES + at] = run
+            run = run + kd[d * PLACES + at]
+        tot[d] = run
+
+        def fill(i, carry, d=d):
+            h, c = carry
+            hc = jnp.minimum(h, PLACES)
+            at = lax.rem(place + (2 * PLACES - hc if d == 0 else hc), PLACES)
+            chunk = jnp.minimum(c + (0 if d == 0 else kd[at]), 7)
+            live = jnp.clip(nn[at] - CHUNK * chunk, 0, CHUNK)
+            slot_rc[d * slots + i] = ring_blk(at) * 8 + chunk
+            slot_live[d * slots + i] = jnp.where(h <= PLACES, live, 0)
+            over = c + 1 >= kd[d * PLACES + at]
+            return jnp.where(over, h + 1, h), jnp.where(over, 0, c + 1)
+
+        lax.fori_loop(0, slots, fill, (jnp.int32(1), jnp.int32(0)))
+
+    own_at = (tot[0] - own_k[0], tot[1] - own_k[1])
+    held[...] = jnp.zeros_like(held)
+    sog_acc[...] = jnp.zeros_like(sog_acc)
+    w_copy.wait()
+
+    def ex_copy(slot, g, o):
+        to = lax.rem(feat + o, FEATS)
+        return pltpu.make_async_remote_copy(
+            src_ref=ex_tx.at[slot, to], dst_ref=ex_rx.at[g, feat], send_sem=ex_ss.at[slot, o - 1],
+            recv_sem=ex_rs.at[g, feat], device_id=(blk, to), device_id_type=MESH)
+
+    def ex_wait(g, o):
+        src = lax.rem(feat + o, FEATS)
+        return pltpu.make_async_remote_copy(
+            src_ref=ex_tx.at[0, src], dst_ref=ex_rx.at[g, src], send_sem=ex_ss.at[0, o - 1],
+            recv_sem=ex_rs.at[g, src], device_id=(blk, src), device_id_type=MESH)
+
+    def gp_copy(g, o):
+        to = lax.rem(feat + o, FEATS)
+        return pltpu.make_async_remote_copy(
+            src_ref=gp.at[g, feat], dst_ref=gp.at[g, feat], send_sem=gp_ss.at[g, o - 1],
+            recv_sem=gp_rs.at[g, feat], device_id=(blk, to), device_id_type=MESH)
+
+    def gp_wait(g, o):
+        src = lax.rem(feat + o, FEATS)
+        return pltpu.make_async_remote_copy(
+            src_ref=gp.at[g, src], dst_ref=gp.at[g, src], send_sem=gp_ss.at[g, o - 1],
+            recv_sem=gp_rs.at[g, src], device_id=(blk, src), device_id_type=MESH)
+
+    def forward(g):
+        slot = lax.rem(g, 2)
+
+        @pl.when(g >= 2)
+        def _():
+            for o in range(1, FEATS):
+                ex_copy(slot, g, o).wait_send()
+
+        for t in range(TOWERS):
+            rows = x[g, t].reshape(2 * SPAN * CHUNK, feats_dim)
+            for h in range(2):
+                out = lax.dot_general(
+                    rows, w[t, 2 * h * quarter:2 * (h + 1) * quarter],
+                    (((1,), (1,)), ((), ())), preferred_element_type=f32)
+                for e in range(2):
+                    ex_tx[slot, 2 * h + e, t] = out[:, e * quarter:(e + 1) * quarter].reshape(
+                        2 * SPAN, CHUNK, quarter)
+        for o in range(1, FEATS):
+            ex_copy(slot, g, o).start()
+        ex_rx[g, feat] = ex_tx[slot, feat]
+
+    bias_here = bias_ref[:, pl.ds(pl.multiple_of(blk * units + feat * quarter, quarter), quarter)]
+
+    def head(g):
+        for o in range(1, FEATS):
+            ex_wait(g, o).wait_recv()
+
+        def one(s, carry):
+            d, ci = lax.div(s, SPAN), lax.rem(s, SPAN)
+            i = g * SPAN + ci
+            rc = slot_rc[d * slots + i]
+            live = slot_live[d * slots + i]
+            mask = jnp.where(
+                lax.broadcasted_iota(i32, (CHUNK, quarter), 0) < live, f32(1), f32(0))
+            act, slope, cot = [], [], []
+            for t in range(TOWERS):
+                pre = ex_rx[g, 0, t, s]
+                for q in range(1, FEATS):
+                    pre = pre + ex_rx[g, q, t, s]
+                pre = pre + bias_here[t:t + 1]
+                square = pre * pre
+                th = jnp.tanh(f32(0.7978845608028654) * (pre + f32(0.044715) * (square * pre)))
+                cdf = f32(0.5) * (f32(1) + th)
+                act.append(pre * cdf)
+                slope.append(cdf + f32(0.5) * pre * (f32(1) - th * th) * (
+                    f32(0.7978845608028654) * (f32(1) + f32(3 * 0.044715) * square)))
+                cot.append(cot_rx[lax.div(rc, 8), lax.rem(rc, 8), t].astype(f32) * mask)
+            for t in range(TOWERS):
+                out = so_ref[2 * t:2 * t + 1] * act[0] + so_ref[2 * t + 1:2 * t + 2] * act[1]
+                acts[i, d, t] = (out * mask).astype(bf16)
+                for u in range(TOWERS):
+                    sog_acc[2 * t + u] = sog_acc[2 * t + u] + cot[t] * act[u]
+            for u in range(TOWERS):
+                back = so_ref[u:u + 1] * cot[0] + so_ref[2 + u:3 + u] * cot[1]
+                gp[g, feat, u, s] = (slope[u] * back).astype(bf16)
+            return carry
+
+        lax.fori_loop(0, 2 * SPAN, one, 0)
+        for o in range(1, FEATS):
+            gp_copy(g, o).start()
+
+    tile = feats_dim // 3
+
+    def backward(g):
+        for o in range(1, FEATS):
+            gp_wait(g, o).wait_recv()
+        for t in range(TOWERS):
+            rows = jnp.concatenate(
+                [gp[g, q, t].reshape(2 * SPAN * CHUNK, quarter) for q in range(FEATS)], axis=1)
+            for n in range(3):
+                part[t, :, :, n * tile:(n + 1) * tile] = jnp.dot(
+                    rows, w[t, :, n * tile:(n + 1) * tile],
+                    preferred_element_type=f32).reshape(2 * SPAN, CHUNK, tile)
+
+    wide = feats_dim // 6
+
+    def wg_copy(q):
+        return pltpu.make_async_copy(
+            wg_tx.at[lax.rem(q, 2)],
+            wg_hbm.at[lax.div(q, 6), :, pl.ds(pl.multiple_of(lax.rem(q, 6) * wide, 128), wide)],
+            wg_sem.at[lax.rem(q, 2)])
+
+    def weight_tile(q):
+        t = lax.div(q, 6)
+        cols = pl.ds(pl.multiple_of(lax.rem(q, 6) * wide, 128), wide)
+
+        @pl.when(q >= 2)
+        def _():
+            wg_copy(q).wait()
+
+        rows = x[0:groups, t, :, :, :, cols].reshape(groups * 2 * SPAN * CHUNK, wide)
+        for e in range(FEATS):
+            grads = gp[0:groups, e, t].reshape(groups * 2 * SPAN * CHUNK, quarter)
+            wg_tx[lax.rem(q, 2), e * quarter:(e + 1) * quarter] = lax.dot_general(
+                grads, rows, (((0,), (0,)), ((), ())), preferred_element_type=f32)
+        wg_copy(q).start()
+
+    def gather_unit(g, q):
+        u = 2 * SPAN * g + q
+        ci, t = lax.div(q, 2), lax.rem(q, 2)
+        i = SPAN * g + ci
+        for d in (0, 1):
+            c = jnp.clip(i - own_at[d], 0, own_k[d] - 1) + own_base[d]
+            own = x[groups, t, lax.div(c, SPAN), lax.rem(c, SPAN)]
+
+            @pl.when(u < sent)
+            def _(d=d, own=own):
+                ring_unit_copy(d, u).wait_recv()
+                x[g, t, d, ci] = jnp.where(i >= own_at[d], own, land[d, u])
+
+            @pl.when(u >= sent)
+            def _(d=d, own=own):
+                x[g, t, d, ci] = own
+
+        m = u + 2
+        for d in (0, 1):
+            @pl.when(m < sent)
+            def _(d=d):
+                @pl.when(m >= 4)
+                def _():
+                    ring_unit_copy(d, m).wait_send()
+
+                im = i + 1
+                here = im < own_k[d]
+                cm = jnp.minimum(im, own_k[d] - 1) + own_base[d]
+                src = jnp.maximum(im - own_k[d], 0)
+                ring_tx[d, lax.rem(m, 4)] = x[
+                    jnp.where(here, groups, lax.div(src, SPAN)), t,
+                    jnp.where(here, lax.div(cm, SPAN), d),
+                    jnp.where(here, lax.rem(cm, SPAN), lax.rem(src, SPAN))]
+                ring_unit_copy(d, m).start()
+
+    def sum_copy(d, v):
+        return pltpu.make_async_remote_copy(
+            src_ref=sums.at[d, v], dst_ref=sum_rx.at[d, v], send_sem=rs_ss.at[d, v],
+            recv_sem=rs_rs.at[d, v], device_id=(ring_to[d], feat), device_id_type=MESH)
+
+    def sum_unit(g, q):
+        v = 2 * SPAN * g + q
+        ci, t = lax.div(q, 2), lax.rem(q, 2)
+        for d in (0, 1):
+            @pl.when(jnp.logical_and(v >= 2, v - 2 < sent))
+            def _(d=d):
+                sum_copy(d, v - 2).wait_recv()
+                held[d, lax.rem(v - 2, 8)] = sum_rx[d, v - 2]
+
+            came = held[d, lax.rem(v - 2 * prev_k[d] + 8, 8)].astype(f32)
+            value = part[t, d * SPAN + ci] + came * jnp.where(v >= 2 * prev_k[d], f32(1), f32(0))
+            sums[d, v] = value.astype(bf16)
+
+            @pl.when(v < sent)
+            def _(d=d):
+                sum_copy(d, v).start()
+
+    def act_copy(r):
+        return pltpu.make_async_remote_copy(
+            src_ref=act_tx.at[r], dst_ref=act_rx.at[half_at], send_sem=act_ss.at[r],
+            recv_sem=act_rs.at[half_at], device_id=(r, row_feat), device_id_type=MESH)
+
+    def act_wait(s):
+        return pltpu.make_async_remote_copy(
+            src_ref=act_tx.at[0], dst_ref=act_rx.at[s], send_sem=act_ss.at[0],
+            recv_sem=act_rs.at[s], device_id=(blk, feat), device_id_type=MESH)
+
+    def sog_copy(r):
+        return pltpu.make_async_remote_copy(
+            src_ref=sog_tx, dst_ref=sog_rx.at[half_at], send_sem=sog_ss.at[r],
+            recv_sem=sog_rs.at[half_at], device_id=(r, row_feat), device_id_type=MESH)
+
+    def sog_wait(s):
+        return pltpu.make_async_remote_copy(
+            src_ref=sog_tx, dst_ref=sog_rx.at[s], send_sem=sog_ss.at[0],
+            recv_sem=sog_rs.at[s], device_id=(blk, feat), device_id_type=MESH)
+
+    def send_acts():
+        sog_tx[...] = jnp.concatenate(
+            [jnp.sum(sog_acc[e], axis=0, keepdims=True) for e in range(4)] * 2, axis=0)
+
+        def pick(rc, carry):
+            r, c = lax.div(rc, 8), lax.rem(rc, 8)
+            at = ring_place(r)
+            first, second = kd[at], kd[PLACES + at]
+            d = jnp.where(c >= first, 1, 0)
+            i = jnp.minimum(start[d * PLACES + at] + c - d * first, slots - 1)
+            keep = jnp.where(c < first + second, f32(1), f32(0))
+            for t in range(TOWERS):
+                act_tx[r, c, t] = (acts[i, d, t].astype(f32) * keep).astype(bf16)
+            return carry
+
+        lax.fori_loop(0, PLACES * 8, pick, 0)
+
+        def send(r, carry):
+            @pl.when(near_not_me(r))
+            def _():
+                act_copy(r).start()
+                sog_copy(r).start()
+
+            @pl.when(jnp.logical_not(near_not_me(r)))
+            def _():
+                act_rx[half_at] = act_tx[r]
+                sog_rx[half_at] = sog_tx[...]
+
+            return carry
+
+        lax.fori_loop(0, PLACES, send, 0)
+
+    def iteration(it, carry):
+        @pl.when(it >= 3)
+        def _():
+            backward(it - 3)
+
+        @pl.when(it == 2)
+        def _():
+            def arrived(r, carry):
+                @pl.when(near_not_me(r))
+                def _():
+                    cot_wait(r).wait_recv()
+
+                return carry
+
+            lax.fori_loop(0, PLACES, arrived, 0)
+
+        @pl.when(jnp.logical_and(it >= 2, it < groups + 2))
+        def _():
+            head(it - 2)
+
+        @pl.when(jnp.logical_and(it >= 1, it < groups + 1))
+        def _():
+            forward(it - 1)
+
+        @pl.when(it == groups + 1)
+        def _():
+            send_acts()
+
+        def unit(q, carry):
+            @pl.when(it < groups)
+            def _():
+                gather_unit(it, q)
+
+            @pl.when(it >= 3)
+            def _():
+                sum_unit(it - 3, q)
+
+            @pl.when(jnp.logical_and(it == groups + 2, q < 6))
+            def _():
+                weight_tile(2 * q)
+                weight_tile(2 * q + 1)
+
+            return carry
+
+        lax.fori_loop(0, 2 * SPAN, unit, 0)
+        return carry
+
+    lax.fori_loop(0, groups + 3, iteration, 0)
+
+    for c in range(8):
+        d = jnp.where(c >= own_k[0], 1, 0)
+        i = jnp.where(c >= own_k[0], own_at[1] + c - own_k[0], own_at[0] + c)
+        i = jnp.clip(i, 0, slots - 1)
+        keep = jnp.where(c < own_k[0] + own_k[1], f32(1), f32(0))
+        for t in range(TOWERS):
+            gf_out[c, t] = (sums[d, 2 * i + t].astype(f32) * keep).astype(bf16)
+
+    for e in range(FEATS):
+        for t in range(TOWERS):
+            def add(g, total, e=e, t=t):
+                return total + jnp.sum(gp[g, e, t].astype(f32), axis=0)
+
+            total = lax.fori_loop(0, groups, add, jnp.zeros((CHUNK, quarter), f32))
+            bg_out[t:t + 1, e * quarter:(e + 1) * quarter] = jnp.sum(total, axis=0, keepdims=True)
+
+    def finish(s, carry):
+        @pl.when(far_not_me(s))
+        def _():
+            act_wait(s).wait_recv()
+            sog_wait(s).wait_recv()
+            cot_copy(s).wait_send()
+
+        @pl.when(near_not_me(s))
+        def _():
+            act_copy(s).wait_send()
+            sog_copy(s).wait_send()
+
+        return carry
+
+    lax.fori_loop(0, 8, finish, 0)
+    act_out[...] = act_rx[...]
+    sog_out[...] = sog_rx[...]
+
+    def finish_sums(v, carry):
+        for d in (0, 1):
+            sum_copy(d, v).wait_send()
+        return carry
+
+    lax.fori_loop(0, sent, finish_sums, 0)
+    for m in range(sent - 4, sent):
+        for d in (0, 1):
+            ring_unit_copy(d, jnp.int32(m)).wait_send()
+    for o in range(1, FEATS):
+        for g in (groups - 2, groups - 1):
+            ex_copy(g % 2, g, o).wait_send()
+
+        def finish_gp(g, carry, o=o):
+            gp_copy(g, o).wait_send()
+            return carry
+
+        lax.fori_loop(0, groups, finish_gp, 0)
+    for q in (10, 11):
+        wg_copy(jnp.int32(q)).wait()
+
+
+def fc_layer(steps, number, n, so, bias, x, cot, weight):
+    units, feats_dim = weight.shape[1:]
+    quarter = units // FEATS
+    groups = -(-steps // SPAN)
+    slots = groups * SPAN
+    vm = pltpu.VMEM
+    dma = pltpu.SemaphoreType.DMA
+    sm = pltpu.SMEM
+    unit = (CHUNK, feats_dim)
+    vmem_spec = pl.BlockSpec(memory_space=pltpu.VMEM)
+    any_spec = pl.BlockSpec(memory_space=pl.ANY)
+    rows = 2 * slots * CHUNK
+    return pl.pallas_call(
+        functools.partial(fc_kernel, steps),
+        out_shape=(
+            jax.ShapeDtypeStruct((8, 8, TOWERS, CHUNK, quarter), bf16),
+            jax.ShapeDtypeStruct((8, TOWERS) + unit, bf16),
+            jax.ShapeDtypeStruct(weight.shape, f32),
+            jax.ShapeDtypeStruct((TOWERS, units), f32),
+            jax.ShapeDtypeStruct((8, 8, quarter), f32),
+        ),
+        in_specs=[pl.BlockSpec(memory_space=pltpu.SMEM)] + [vmem_spec] * 4 + [any_spec],
+        out_specs=(vmem_spec, vmem_spec, any_spec, vmem_spec, vmem_spec),
+        scratch_shapes=[
+            vm(weight.shape, bf16),
+            vm((groups + 1, TOWERS, 2, SPAN) + unit, bf16),
+            vm((2, 2 * steps - 2) + unit, bf16),
+            vm((2, 4) + unit, bf16),
+            vm((2, FEATS, TOWERS, 2 * SPAN, CHUNK, quarter), f32),
+            vm((groups, FEATS, TOWERS, 2 * SPAN, CHUNK, quarter), f32),
+            vm((groups, FEATS, TOWERS, 2 * SPAN, CHUNK, quarter), bf16),
+            vm((TOWERS, 2 * SPAN) + unit, f32),
+            vm((2, 2 * steps - 2) + unit, bf16),
+            vm((2, 8) + unit, bf16),
+            vm((2, 2 * slots) + unit, bf16),
+            vm((8, 8, TOWERS, CHUNK, quarter), bf16),
+            vm((slots, 2, TOWERS, CHUNK, quarter), bf16),
+            vm((8, 8, TOWERS, CHUNK, quarter), bf16),
+            vm((8, 8, TOWERS, CHUNK, quarter), bf16),
+            vm((4, CHUNK, quarter), f32),
+            vm((8, quarter), f32),
+            vm((8, 8, quarter), f32),
+            vm((2, units, feats_dim // 6), f32),
+            sm((2 * PLACES,), i32),
+            sm((PLACES,), i32),
+            sm((2 * PLACES,), i32),
+            sm((2,), i32),
+            sm((2 * slots,), i32),
+            sm((2 * slots,), i32),
+            dma,
+            dma((2, 4)),
+            dma((2, 2 * steps - 2)),
+            dma((2, 2 * steps - 2)),
+            dma((2, 2 * steps - 2)),
+            dma((2, 3)),
+            dma((groups, FEATS)),
+            dma((groups, 3)),
+            dma((groups, FEATS)),
+            dma((8,)),
+            dma((8,)),
+            dma((8,)),
+            dma((8,)),
+            dma((8,)),
+            dma((8,)),
+            dma((2,)),
+        ],
+        cost_estimate=pl.CostEstimate(
+            flops=6 * rows * TOWERS * units * feats_dim, bytes_accessed=30 << 20,
+            transcendentals=rows * TOWERS * quarter),
+        compiler_params=pltpu.CompilerParams(
+            collective_id=number, has_side_effects=True, vmem_limit_bytes=60 << 20),
+    )(n, so, bias, x, cot, weight)
+
+
+CLASSES = (20, 24)
+
+
+def body_ring(conv_maps, crop_counts, fc_weight, fc_bias, stitch_in, stitch_out, cotangent):
+    num_rows = conv_maps.shape[0]
+    merged = conv_maps.shape[2]
+    chans = merged // TOWERS
+    units = fc_weight.shape[1]
+    quarter = units // FEATS
+    chunks = num_rows // CHUNK
+    feat_idx = lax.axis_index("feat")
+    blk_idx = lax.axis_index("blk")
+    n = lax.all_gather(jnp.sum(crop_counts), "blk")
+    so = lax.all_gather(stitch_out, "feat", axis=2, tiled=True)
+    so = lax.dynamic_slice_in_dim(so, blk_idx * units + feat_idx * quarter, quarter, 2).reshape(
+        4, quarter)
+    cot = cotangent.reshape(chunks, CHUNK, TOWERS, 8, quarter).transpose(3, 0, 2, 1, 4)
+    sums = jnp.einsum("rpm,pq->rqm", conv_maps, pool_table(bf16), preferred_element_type=f32)
+    pooled = jnp.transpose(sums.reshape(num_rows, GRID * GRID, chans, TOWERS), (0, 3, 2, 1)) * (
+        1.0 / 9.0
+    )
+    mixed, pull_first = jax.vjp(stitch_first, pooled, stitch_in)
+    feats = mixed.astype(bf16).reshape(chunks, CHUNK, TOWERS, -1).transpose(0, 2, 1, 3)
+    need = lax.div(jnp.sum(lax.div(n + (CHUNK - 1), CHUNK)) + 1, 2)
+    full = PLACES * chunks // 2
+    kinds = CLASSES + (full,)
+    pick = sum(((need > c).astype(i32) for c in CLASSES), jnp.int32(0))
+    act, gf, weight_grad, bias_grad, sog = lax.switch(
+        pick,
+        [functools.partial(fc_layer, steps, at) for at, steps in enumerate(kinds)],
+        n, so, fc_bias, feats, cot, fc_weight)
+    activations = act.transpose(1, 3, 2, 0, 4).reshape(num_rows, TOWERS, -1)
+    stitch_out_grad = sog[:, :4].transpose(1, 0, 2).reshape(TOWERS, TOWERS, -1)
+    grad_mixed = gf.transpose(0, 2, 1, 3).astype(f32).reshape(num_rows, TOWERS, chans, -1)
+    grad_pooled, grad_si = pull_first(grad_mixed)
+    spread = jnp.einsum(
+        "rtcq,pq->rpct", grad_pooled * (1.0 / 9.0), pool_table(f32), precision=lax.Precision.HIGHEST
+    )
+    conv_grad = spread.reshape(num_rows, MAP * MAP, merged).astype(bf16)
+    stitch_in_grad = lax.psum(grad_si, "blk")
+    return (activations, conv_grad, weight_grad, bias_grad, stitch_in_grad, stitch_out_grad)
+
+
 def solution(mesh):
+    ring = mesh.shape["blk"] == PLACES and mesh.shape["feat"] == FEATS
     return jax.shard_map(
-        body,
+        body_ring if ring else body_plain,
         mesh=mesh,
         in_specs=(
             P("blk", None, "feat"),

time: 1360 us -> 375 us (0.28)
  waiting for transfers between devices: 909 us -> 0 us
  Pallas kernels: 0 us -> 209 us
  blocking collectives: 225 us -> 55 us
  matrix products: 113 us -> 36.3 us
  starting transfers between devices: 16.7 us -> 0 us
    all_gather x3 -> x0, waiting for transfers between devices: 796 us -> none  [the longest x1 633 us: body(): lax.all_gather(fc_weight, 'blk', axis=1, tiled=True)]
    pallas_call x0 -> x1, Pallas kernels: none -> 209 us  [fc_layer(): pl.pallas_call(functools.partial(fc_kernel, steps), out_shape=(jax.ShapeD...]
    all_to_all x1 -> x0, blocking collectives: 96.3 us -> none  [body(): lax.all_to_all(own_cols, 'blk', split_axis=0, concat_axis=2, tiled=True)]
    psum x1, blocking collectives: 128 us -> 36.5 us  [body_ring(): stitch_in_grad = lax.psum(grad_si, 'blk')]
    unnamed x5 -> x0, waiting for transfers between devices: 71.5 us -> none
    dot_general x8 -> x2, matrix products: 73.1 us -> 11.2 us  [the longest x1 6.06 us: body_ring(): jnp.einsum('rpm,pq->rqm', conv_maps, pool_table(bf16), preferred_element_...]
    all_to_all x1 -> x0, waiting for transfers between devices: 41.7 us -> none  [body(): lax.all_to_all(grad_all, 'blk', split_axis=2, concat_axis=0, tiled=True)]
    reshape x1 -> x6, local copies, waits for them, and re-layouts: 2.7 us -> 23.3 us  [the longest x1 12.2 us: body_ring(): gf.transpose(0, 2, 1, 3).astype(f32).reshape(num_rows, TOWERS, chans, -1)]
  transfers between devices with their start and end apart: 5 -> 0, of which waited for: 5 -> 0; matrix products, arithmetic and copies ran while one was open for 4% -> 0% of each run, Pallas kernels for 0% -> 0%
where the time goes in v1:
time: 375 us; the launch traced here: 379 us
  Pallas kernels  209 us (56%)
  local copies, waits for them, and re-layouts  74.2 us (20%)
  blocking collectives  55 us (15%)
  matrix products  36.3 us (10%)
    pallas_call x1, Pallas kernels, fc_layer(): pl.pallas_call(functools.partial(fc_kernel, steps), out_shape=(jax.ShapeD...  209 us
    psum x1, blocking collectives, body_ring(): stitch_in_grad = lax.psum(grad_si, 'blk')  36.5 us
    dot_general x3, matrix products, stitch_first(): jnp.einsum('tuc,rucq->rtcq', stitch_in, pooled, precision=lax.Precision.H...  25 us
    unnamed x18, local copies, waits for them, and re-layouts  20.9 us
    unnamed x1, blocking collectives  13.1 us
    convert_element_type x1, local copies, waits for them, and re-layouts, body_ring(): conv_grad = spread.reshape(num_rows, MAP * MAP, merged).astype(bf16)  13 us
    reshape x1, local copies, waits for them, and re-layouts, body_ring(): gf.transpose(0, 2, 1, 3).astype(f32).reshape(num_rows, TOWERS, chans, -1)  12.2 us
    reshape x1, local copies, waits for them, and re-layouts, body_ring(): mixed.astype(bf16).reshape(chunks, CHUNK, TOWERS, -1).transpose(0, 2, 1, 3)  8.09 us

profile of v1, /device:TPU:0, one launch (start us, length us, event | category | flops | bytes accessed | tf_op | source)
XLA Modules:
  0.0 378.5 jit_solution(62615402998361419)
XLA Ops:
  0.6 1.2 dynamic-slice
  1.9 1.3 reduce_sum.18
  3.2 1.4 dynamic-update-slice
  4.6 13.1 %all-reduce = s32[8]{0:T(128)S(1)} all-reduce(s32[8]{0:T(128)S(1)} %dynamic-update-slice), channel_id=1, replica_groups=mesh['blk'=8,'feat'=4] {'blk'}, use_global_device_ids=true, to_apply=%add | all-reduce | flops 8 | bytes 64
  17.6 0.6 fusion.31
  19.0 0.0 copy-start.2
  19.0 0.8 copy.40
  19.8 0.0 copy-start.1
  19.8 5.5 %all_gather.11 = f32[2,2,4096]{2,1,0:T(2,128)S(1)} all-gather(f32[2,2,1024]{2,1,0:T(2,128)} %param.15), channel_id=1, replica_groups=mesh['blk'=8,'feat'=4] {'feat'}, dimensions={2}, use_global_device_ids=true | all-gather | bytes 81920 | tf_op jit(solution)/shard_map/all_gather | solution.py:672
  25.2 1.4 reshape.93
  26.6 0.1 copy.67
  26.8 6.1 %multiply_bitcast_fusion = f32[128,36,128]{2,1,0:T(8,128)S(1)} fusion(bf16[128,169,128]{2,0,1:T(8,128)(2,1)} %param.10, s32[36]{0:T(128)S(1)} %get-tuple-element.102, s32[169]{0:T(256)S(1)} %get-tuple-element.100, s32[36]{0:T(128)S(1)} %get-tuple-element.103, s32[169]{0:T(256)S(1)} %get-tuple-element.101), kind=kOutput, calls=%fused_computation.5 | convolution fusion | flops 200005088 | bytes 7898728 | tf_op jit(solution)/shard_map/rpm,pq->rqm/dot_general | solution.py:676
  32.8 0.0 copy-done.2
  32.8 2.1 copy.21
  34.9 0.0 copy-done.1
  34.9 9.7 %fusion.12 = bf16[128,2,64,36]{0,1,3,2:T(2,128)(2,1)S(1)} fusion(f32[2,2,64,1]{1,0,3,2:T(2,128)S(1)} %copy.40, f32[128,2,64,36]{0,1,2,3:T(2,128)} %bitcast.62), kind=kOutput, calls=%fused_computation.11 | convolution fusion | flops 14745600 | bytes 3539968 | tf_op jit(solution)/shard_map/jvp(tuc,rucq->rtcq)/dot_general | solution.py:38
  44.6 4.8 %copy.24 = bf16[128,2,64,36]{3,2,0,1:T(8,128)(2,1)} copy(bf16[128,2,64,36]{0,1,3,2:T(2,128)(2,1)S(1)} %fusion.12) | data formatting | bytes 2359296 | tf_op jit(solution)/shard_map/convert_element_type | solution.py:681
  49.5 0.0 copy-start.4
  49.5 8.1 %reshape.78 = bf16[8,16,2,2304]{3,1,0,2:T(8,128)(2,1)S(1)} reshape(bf16[128,2,64,36]{3,2,0,1:T(8,128)(2,1)} %copy.24) | data formatting | bytes 2359296 | tf_op jit(solution)/shard_map/reshape | solution.py:681
  57.6 0.0 copy-done.4
  57.6 211.2 %conditional.1 = ((bf16[8,8,2,16,128]{4,3,2,1,0:T(8,128)(2,1)}, bf16[8,2,16,2304]{3,2,1,0:T(8,128)(2,1)S(1)}, f32[2,512,2304]{2,1,0:T(8,128)}, f32[2,512]{1,0:T(2,128)S(1)}, f32[8,8,128]{2,1,0:T(8,128)S(1)})) conditional(s32[]{:T(128)} %clamp.3, (s32[8]{0:T(128)S(1)}, f32[4,128]{1,0:T(4,128)S(1)}, f32[2,4096]{1,0:T(2,128)S(1)}, ...), branch_computations={%region_2.3_spmd, %region_3.4_spmd, %region_4.5_spmd} | conditional | flops 14495514624 | bytes 34865160 | solution.py:686
  57.8 0.9 copy.29.cot_ref
  58.7 1.1 copy.28.x_ref
  59.8 208.8 %branch_1_fun.1 = (bf16[8,8,2,16,128]{4,3,2,1,0:T(8,128)(2,1)}, bf16[8,2,16,2304]{3,2,1,0:T(8,128)(2,1)S(1)}, f32[2,512,2304]{2,1,0:T(8,128)}, f32[2,512]{1,0:T(2,128)S(1)}, f32[8,8,128]{2,1,0:T(8,128)S(1)}) custom-call(s32[8]{0:T(128)S(1)} %get-tuple-element.42.n_ref, f32[4,128]{1,0:T(4,128)S(1)} %get-tuple-element.43.so_ref, ...), custom_call_target="tpu_custom_call" | custom-call | flops 10871635968 | bytes 31457280 | tf_op jit(solution)/shard_map/cond/branch_1_fun/pallas_call | solution.py:597
  268.8 1.4 copy.32
  270.1 0.9 reshape.80
  271.1 0.1 copy.33
  271.2 0.6 reshape.82
  271.8 12.2 %reshape.81 = bf16[128,2,64,36]{3,2,0,1:T(8,128)(2,1)} reshape(bf16[8,16,2,2304]{3,1,0,2:T(8,128)(2,1)S(1)} %copy.33) | data formatting | bytes 2359296 | tf_op jit(solution)/shard_map/reshape | solution.py:692
  284.0 0.0 copy-start
  284.0 6.6 %copy.35 = bf16[64,128,36,2]{1,3,2,0:T(2,128)(2,1)S(1)} copy(bf16[64,128,36,2]{2,0,1,3:T(8,128)(2,1)} %bitcast.58) | data formatting | bytes 2359296 | tf_op jit(solution)/shard_map/transpose(jvp(tuc,rucq->rtcq))/transpose | solution.py:38
  290.6 0.0 copy-done
  290.6 10.3 %fusion.16 = f32[2,2,64]{1,0,2:T(2,128)} fusion(bf16[64,128,36,2]{1,3,2,0:T(2,128)(2,1)S(1)} %copy.35, f32[128,2,64,36]{0,1,2,3:T(2,128)S(1)} %bitcast.63), kind=kOutput, calls=%fused_computation.13 | convolution fusion | flops 14155776 | bytes 3539968 | tf_op jit(solution)/shard_map/transpose(jvp(tuc,rucq->rtcq))/dot_general | solution.py:38
  300.9 36.5 %psum.7 = f32[2,2,64]{1,0,2:T(2,128)S(1)} all-reduce(f32[2,2,64]{1,0,2:T(2,128)} %fusion.16), channel_id=1, replica_groups=mesh['blk'=8,'feat'=4] {'blk'}, use_global_device_ids=true, to_apply=%region_5.6 | all-reduce | flops 256 | bytes 2048 | tf_op jit(solution)/shard_map/psum | solution.py:698
  337.4 0.0 copy-start.3
  337.4 0.7 copy.39
  338.0 5.1 %fusion.37 = f32[64,128,36,2]{1,3,2,0:T(2,128)S(1)} fusion(bf16[64,128,36,2]{1,3,2,0:T(2,128)(2,1)S(1)} %copy.35, f32[2,2,64,1]{1,0,3,2:T(2,128)} %copy-done.1), kind=kOutput, calls=%fused_computation.49 | convolution fusion | flops 14155776 | bytes 3539968 | tf_op jit(solution)/shard_map/transpose(jvp(tuc,rucq->rtcq))/dot_general | solution.py:38
  343.1 0.0 copy-done.3
  343.1 5.2 %convert_bitcast_fusion = bf16[128,169,64,2]{0,1,2,3:T(8,128)(2,1)S(1)} fusion(f32[64,128,36,2]{1,3,2,0:T(2,128)S(1)} %fusion.37, s32[36]{0:T(128)S(1)} %get-tuple-element.102, s32[169]{0:T(256)S(1)} %get-tuple-element.100, s32[36]{0:T(128)S(1)} %copy-done.3, s32[169]{0:T(256)S(1)} %get-tuple-element.101), kind=kOutput, calls=%fused_computation.2 | convolution fusion | flops 1199576576 | bytes 7898728 | tf_op jit(solution)/shard_map/rtcq,pq->rpct/dot_general | solution.py:694
  348.3 13.0 %copy.34 = bf16[128,169,64,2]{0,3,2,1:T(2,128)(2,1)} copy(bf16[128,169,64,2]{0,1,2,3:T(8,128)(2,1)S(1)} %convert_bitcast_fusion) | data formatting | bytes 11075584 | tf_op jit(solution)/shard_map/convert_element_type | solution.py:697
  361.3 8.2 %copy.38 = bf16[128,169,128]{2,0,1:T(8,128)(2,1)} copy(bf16[128,169,128]{0,2,1:T(8,128)(2,1)} %bitcast.54) | data formatting | bytes 11075584
  369.5 8.0 %copy.86 = f32[2,512,2304]{2,1,0:T(8,128)} copy(f32[2,512,2304]{2,1,0:T(8,128)} %get-tuple-element.127) | data formatting | bytes 18874368
  377.5 0.6 copy.87
  (6 shorter events, 0.0 us)
Async XLA Ops:
  19.0 13.9 %copy-start.2 = (s32[36]{0:T(128)}, s32[36]{0:T(128)S(1)}, u32[]{:S(2)}) copy-start(s32[36]{0:T(128)S(1)} %get-tuple-element.103) | copy-start | bytes 436
  19.8 15.1 %copy-start.1 = (f32[2,2,64,1]{1,0,3,2:T(2,128)}, f32[2,2,64,1]{1,0,3,2:T(2,128)S(1)}, u32[]{:S(2)}) copy-start(f32[2,2,64,1]{1,0,3,2:T(2,128)S(1)} %copy.40) | copy-start | bytes 3076
  49.5 8.1 %copy-start.4 = (f32[2,4096]{1,0:T(2,128)S(1)}, f32[2,4096]{1,0:T(2,128)}, u32[]{:S(2)}) copy-start(f32[2,4096]{1,0:T(2,128)} %param.13) | copy-start | bytes 98308
  284.0 6.6 %copy-start = (f32[128,36,128]{0,2,1:T(8,128)S(1)}, f32[128,36,128]{0,2,1:T(8,128)}, u32[]{:S(2)}) copy-start(f32[128,36,128]{0,2,1:T(8,128)} %copy.21) | copy-start | bytes 7077892
  337.4 5.7 %copy-start.3 = (s32[36]{0:T(128)S(1)}, s32[36]{0:T(128)}, u32[]{:S(2)}) copy-start(s32[36]{0:T(128)} %copy-done.2) | copy-start | bytes 436

commit v2 on v1

--- a/solution.py
+++ b/solution.py
@@ -2,6 +2,7 @@
 
 import jax
 import jax.numpy as jnp
+import numpy as np
 from jax import lax
 from jax.experimental import pallas as pl
 from jax.experimental.pallas import tpu as pltpu
@@ -656,6 +657,312 @@
     )(n, so, bias, x, cot, weight)
 
 
+def layout_matrix(chans):
+    table = np.zeros((4 * 2 * chans, 4 * 2 * chans), np.float32)
+    for q0 in range(4):
+        for c in range(chans):
+            for t in range(TOWERS):
+                lane = 4 * ((9 * c) % 32) + q0
+                table[q0 * 2 * chans + 2 * c + t, (2 * t + c // 32) * 128 + lane] = 1
+    return table
+
+
+def swap_pairs(value):
+    lane = lax.broadcasted_iota(i32, value.shape, value.ndim - 1)
+    return jnp.where(
+        lax.rem(lane, 2) == 0, pltpu.roll(value, 127, value.ndim - 1),
+        pltpu.roll(value, 1, value.ndim - 1))
+
+
+def entry_kernel(
+    cc_ref, so_ref, s_ref, perm_ref, conv_ref,
+    feats_out, pooled_out, n_out, so_out,
+    n_tx, n_rx, so_tx, so_rx, n_ss, n_rs, so_ss, so_rs,
+):
+    blk, feat = lax.axis_index("blk"), lax.axis_index("feat")
+    step = pl.program_id(0)
+    holds = lax.div(blk, 2) == feat
+
+    def n_copy(o):
+        to = lax.rem(blk + o, PLACES)
+        return pltpu.make_async_remote_copy(
+            src_ref=n_tx, dst_ref=n_rx.at[blk], send_sem=n_ss.at[o - 1], recv_sem=n_rs.at[blk],
+            device_id=(to, feat), device_id_type=MESH)
+
+    def n_wait(o):
+        src = lax.rem(blk + o, PLACES)
+        return pltpu.make_async_remote_copy(
+            src_ref=n_tx, dst_ref=n_rx.at[src], send_sem=n_ss.at[o - 1], recv_sem=n_rs.at[src],
+            device_id=(src, feat), device_id_type=MESH)
+
+    def so_copy(o):
+        to = lax.rem(feat + o, FEATS)
+        return pltpu.make_async_remote_copy(
+            src_ref=so_tx.at[to], dst_ref=so_rx, send_sem=so_ss.at[o - 1], recv_sem=so_rs,
+            device_id=(blk, to), device_id_type=MESH)
+
+    @pl.when(step == 0)
+    def _():
+        bar = pltpu.get_barrier_semaphore()
+        for o in range(1, PLACES):
+            pl.semaphore_signal(
+                bar, inc=1, device_id=(lax.rem(blk + o, PLACES), feat), device_id_type=MESH)
+        for o in range(1, FEATS):
+            pl.semaphore_signal(
+                bar, inc=1, device_id=(blk, lax.rem(feat + o, FEATS)), device_id_type=MESH)
+        total = cc_ref[0]
+        for e in range(1, cc_ref.shape[0]):
+            total = total + cc_ref[e]
+        n_tx[...] = jnp.full(n_tx.shape, total, i32)
+        n_rx[blk] = n_tx[...]
+        for q in range(FEATS):
+            at = pl.ds(pl.multiple_of(lax.rem(blk, 2) * 512 + q * 128, 128), 128)
+            for t in range(TOWERS):
+                so_tx[q, 2 * t:2 * t + 2] = so_ref[t, :, at]
+                so_tx[q, 4 + 2 * t:6 + 2 * t] = so_ref[t, :, at]
+        pl.semaphore_wait(bar, PLACES - 1 + FEATS - 1)
+        for o in range(1, PLACES):
+            n_copy(o).start()
+
+        @pl.when(holds)
+        def _():
+            so_rx[...] = so_tx[feat]
+            for o in range(1, FEATS):
+                so_copy(o).start()
+
+    across = {}
+    for row in range(MAP):
+        line = [conv_ref[MAP * row + col].astype(f32) for col in range(MAP)]
+        for v in range(GRID):
+            across[row, v] = line[2 * v] + line[2 * v + 1] + line[2 * v + 2]
+    own, other = s_ref[0:1], s_ref[1:2]
+    parts = []
+    for q1 in range(9):
+        here = []
+        for q0 in range(4):
+            q = 4 * q1 + q0
+            u, v = q // GRID, q % GRID
+            pooled = (across[2 * u, v] + across[2 * u + 1, v] + across[2 * u + 2, v]) * f32(1 / 9)
+            pooled_out[0, q] = pooled
+            here.append((own * pooled + other * swap_pairs(pooled)).astype(bf16))
+        parts.append(jnp.concatenate(here, axis=1))
+    spread = jnp.dot(
+        jnp.concatenate(parts, axis=0), perm_ref[...], preferred_element_type=f32)
+    slot = lax.div(lax.broadcasted_iota(i32, (CHUNK, 128), 1), 4)
+    for t in range(TOWERS):
+        for half in range(2):
+            at = (2 * t + half) * 128
+            turned = [
+                pltpu.roll(spread[q1 * CHUNK:(q1 + 1) * CHUNK, at:at + 128], 4 * q1, 1)
+                if q1 else spread[0:CHUNK, at:at + 128] for q1 in range(9)]
+            for j in range(9):
+                source = lax.rem(slot + 32 * j, 9)
+                tile = turned[0]
+                for q1 in range(1, 9):
+                    tile = jnp.where(source == q1, turned[q1], tile)
+                feats_out[0, t, :, (9 * half + j) * 128:(9 * half + j + 1) * 128] = tile.astype(bf16)
+
+    @pl.when(step == pl.num_programs(0) - 1)
+    def _():
+        for o in range(1, PLACES):
+            n_wait(o).wait_recv()
+            n_copy(o).wait_send()
+
+        @pl.when(holds)
+        def _():
+            for o in range(1, FEATS):
+                so_copy(o).wait_send()
+
+        @pl.when(jnp.logical_not(holds))
+        def _():
+            so_copy(1).wait_recv()
+
+        n_out[...] = n_rx[...]
+        so_out[...] = so_rx[...]
+
+
+def exit_kernel(
+    s_ref, perm_ref, gf_ref, pooled_ref, wg_ref, conv_out, si_out, wg_out, acc,
+):
+    step = pl.program_id(0)
+
+    @pl.when(step == 0)
+    def _():
+        acc[...] = jnp.zeros_like(acc)
+
+    wg_out[...] = wg_ref[...]
+    slot = lax.div(lax.broadcasted_iota(i32, (CHUNK, 128), 1), 4)
+    columns = []
+    for t in range(TOWERS):
+        for half in range(2):
+            tiles = [
+                gf_ref[0, t, :, (9 * half + j) * 128:(9 * half + j + 1) * 128].astype(f32)
+                for j in range(9)]
+            turned = []
+            for q1 in range(9):
+                source = lax.rem(2 * (q1 - slot) + 72, 9)
+                tile = tiles[0]
+                for j in range(1, 9):
+                    tile = jnp.where(source == j, tiles[j], tile)
+                turned.append(pltpu.roll(tile, 128 - 4 * q1, 1) if q1 else tile)
+            columns.append(jnp.concatenate(turned, axis=0).astype(bf16))
+    grads = lax.dot_general(
+        jnp.concatenate(columns, axis=1), perm_ref[...], (((1,), (1,)), ((), ())),
+        preferred_element_type=f32)
+    own, other = s_ref[0:1] * f32(1 / 9), s_ref[2:3] * f32(1 / 9)
+    same = jnp.zeros((CHUNK, 128), f32)
+    cross = jnp.zeros((CHUNK, 128), f32)
+    back = {}
+    for q in range(GRID * GRID):
+        q1, q0 = q // 4, q % 4
+        grad = grads[q1 * CHUNK:(q1 + 1) * CHUNK, q0 * 128:(q0 + 1) * 128]
+        pooled = pooled_ref[0, q]
+        swapped = swap_pairs(grad)
+        same = same + grad * pooled
+        cross = cross + swapped * pooled
+        back[q // GRID, q % GRID] = own * grad + other * swapped
+    acc[0] = acc[0] + same
+    acc[1] = acc[1] + cross
+    lines = []
+    for u in range(GRID):
+        line = []
+        for col in range(MAP):
+            v = col // 2
+            if col % 2:
+                line.append(back[u, v])
+            elif col == 0:
+                line.append(back[u, 0])
+            elif col == MAP - 1:
+                line.append(back[u, GRID - 1])
+            else:
+                line.append(back[u, v - 1] + back[u, v])
+        lines.append(line)
+    for row in range(MAP):
+        u = row // 2
+        for col in range(MAP):
+            if row % 2 or row == 0:
+                value = lines[u][col]
+            elif row == MAP - 1:
+                value = lines[GRID - 1][col]
+            else:
+                value = lines[u - 1][col] + lines[u][col]
+            conv_out[MAP * row + col] = value.astype(bf16)
+
+    @pl.when(step == pl.num_programs(0) - 1)
+    def _():
+        sums = [jnp.sum(acc[e], axis=0, keepdims=True) for e in range(2)]
+        si_out[...] = jnp.concatenate(sums * 4, axis=0)
+
+
+def total_kernel(x_ref, out, rx, ss, rs):
+    blk, feat = lax.axis_index("blk"), lax.axis_index("feat")
+
+    def copy(o):
+        return pltpu.make_async_remote_copy(
+            src_ref=x_ref, dst_ref=rx.at[blk], send_sem=ss.at[o - 1], recv_sem=rs.at[blk],
+            device_id=(lax.rem(blk + o, PLACES), feat), device_id_type=MESH)
+
+    def wait(o):
+        src = lax.rem(blk + o, PLACES)
+        return pltpu.make_async_remote_copy(
+            src_ref=x_ref, dst_ref=rx.at[src], send_sem=ss.at[o - 1], recv_sem=rs.at[src],
+            device_id=(src, feat), device_id_type=MESH)
+
+    bar = pltpu.get_barrier_semaphore()
+    for o in range(1, PLACES):
+        pl.semaphore_signal(
+            bar, inc=1, device_id=(lax.rem(blk + o, PLACES), feat), device_id_type=MESH)
+    pl.semaphore_wait(bar, PLACES - 1)
+    for o in range(1, PLACES):
+        copy(o).start()
+    rx[blk] = x_ref[...]
+    for o in range(1, PLACES):
+        wait(o).wait_recv()
+    total = rx[0]
+    for q in range(1, PLACES):
+        total = total + rx[q]
+    out[...] = total
+    for o in range(1, PLACES):
+        copy(o).wait_send()
+
+
+def entry(counts, so, s_rows, conv):
+    spots, rows, merged = conv.shape
+    chunks = rows // CHUNK
+    chans = merged // TOWERS
+    wide = chans * GRID * GRID
+    vm, dma = pltpu.VMEM, pltpu.SemaphoreType.DMA
+    whole = pl.BlockSpec(memory_space=pltpu.VMEM)
+    return pl.pallas_call(
+        entry_kernel,
+        grid=(chunks,),
+        out_shape=(
+            jax.ShapeDtypeStruct((chunks, TOWERS, CHUNK, wide), bf16),
+            jax.ShapeDtypeStruct((chunks, GRID * GRID, CHUNK, merged), f32),
+            jax.ShapeDtypeStruct((PLACES, 8, 128), i32),
+            jax.ShapeDtypeStruct((8, 128), f32),
+        ),
+        in_specs=[pl.BlockSpec(memory_space=pltpu.SMEM)] + [whole] * 3 + [
+            pl.BlockSpec((spots, CHUNK, merged), lambda c: (0, c, 0))],
+        out_specs=(
+            pl.BlockSpec((1, TOWERS, CHUNK, wide), lambda c: (c, 0, 0, 0)),
+            pl.BlockSpec((1, GRID * GRID, CHUNK, merged), lambda c: (c, 0, 0, 0)),
+            whole, whole,
+        ),
+        scratch_shapes=[
+            vm((8, 128), i32), vm((PLACES, 8, 128), i32), vm((FEATS, 8, 128), f32), vm((8, 128), f32),
+            dma((PLACES - 1,)), dma((PLACES,)), dma((FEATS - 1,)), dma,
+        ],
+        cost_estimate=pl.CostEstimate(flops=1 << 30, bytes_accessed=10 << 20, transcendentals=0),
+        compiler_params=pltpu.CompilerParams(
+            collective_id=8, has_side_effects=True, vmem_limit_bytes=40 << 20),
+    )(counts, so, s_rows, jnp.asarray(layout_matrix(chans), bf16), conv)
+
+
+def leave(s_rows, gf, pooled, weight_grad, spots):
+    chunks, towers, _, wide = gf.shape
+    merged = pooled.shape[-1]
+    vm = pltpu.VMEM
+    whole = pl.BlockSpec(memory_space=pltpu.VMEM)
+    share = pl.BlockSpec(
+        (towers, weight_grad.shape[1] // chunks, wide), lambda c: (0, c, 0))
+    return pl.pallas_call(
+        exit_kernel,
+        grid=(chunks,),
+        out_shape=(
+            jax.ShapeDtypeStruct((spots, chunks * CHUNK, merged), bf16),
+            jax.ShapeDtypeStruct((8, 128), f32),
+            jax.ShapeDtypeStruct(weight_grad.shape, f32),
+        ),
+        in_specs=[whole] * 2 + [
+            pl.BlockSpec((1, towers, CHUNK, wide), lambda c: (c, 0, 0, 0)),
+            pl.BlockSpec((1, GRID * GRID, CHUNK, merged), lambda c: (c, 0, 0, 0)),
+            share],
+        out_specs=(
+            pl.BlockSpec((spots, CHUNK, merged), lambda c: (0, c, 0)),
+            whole, share,
+        ),
+        scratch_shapes=[vm((2, CHUNK, 128), f32)],
+        cost_estimate=pl.CostEstimate(flops=1 << 30, bytes_accessed=30 << 20, transcendentals=0),
+        compiler_params=pltpu.CompilerParams(vmem_limit_bytes=40 << 20),
+    )(s_rows, jnp.asarray(layout_matrix(merged // TOWERS), bf16), gf, pooled, weight_grad)
+
+
+def total_over_blk(value):
+    whole = pl.BlockSpec(memory_space=pltpu.VMEM)
+    dma = pltpu.SemaphoreType.DMA
+    return pl.pallas_call(
+        total_kernel,
+        out_shape=jax.ShapeDtypeStruct(value.shape, f32),
+        in_specs=[whole],
+        out_specs=whole,
+        scratch_shapes=[
+            pltpu.VMEM((PLACES,) + value.shape, f32), dma((PLACES - 1,)), dma((PLACES,))],
+        compiler_params=pltpu.CompilerParams(
+            collective_id=9, has_side_effects=True, vmem_limit_bytes=16 << 20),
+    )(value)
+
+
 CLASSES = (20, 24)
 
 
@@ -666,19 +973,14 @@
     units = fc_weight.shape[1]
     quarter = units // FEATS
     chunks = num_rows // CHUNK
-    feat_idx = lax.axis_index("feat")
-    blk_idx = lax.axis_index("blk")
-    n = lax.all_gather(jnp.sum(crop_counts), "blk")
-    so = lax.all_gather(stitch_out, "feat", axis=2, tiled=True)
-    so = lax.dynamic_slice_in_dim(so, blk_idx * units + feat_idx * quarter, quarter, 2).reshape(
-        4, quarter)
+    own = jnp.stack([stitch_in[0, 0], stitch_in[1, 1]], 1).reshape(1, -1)
+    other = jnp.stack([stitch_in[0, 1], stitch_in[1, 0]], 1).reshape(1, -1)
+    back = jnp.stack([stitch_in[1, 0], stitch_in[0, 1]], 1).reshape(1, -1)
+    s_rows = jnp.concatenate([own, other, back, own], 0)
+    feats, pooled, counts, so = entry(
+        crop_counts, stitch_out, s_rows, conv_maps.transpose(1, 0, 2))
+    n = counts[:, 0, 0]
     cot = cotangent.reshape(chunks, CHUNK, TOWERS, 8, quarter).transpose(3, 0, 2, 1, 4)
-    sums = jnp.einsum("rpm,pq->rqm", conv_maps, pool_table(bf16), preferred_element_type=f32)
-    pooled = jnp.transpose(sums.reshape(num_rows, GRID * GRID, chans, TOWERS), (0, 3, 2, 1)) * (
-        1.0 / 9.0
-    )
-    mixed, pull_first = jax.vjp(stitch_first, pooled, stitch_in)
-    feats = mixed.astype(bf16).reshape(chunks, CHUNK, TOWERS, -1).transpose(0, 2, 1, 3)
     need = lax.div(jnp.sum(lax.div(n + (CHUNK - 1), CHUNK)) + 1, 2)
     full = PLACES * chunks // 2
     kinds = CLASSES + (full,)
@@ -689,13 +991,12 @@
         n, so, fc_bias, feats, cot, fc_weight)
     activations = act.transpose(1, 3, 2, 0, 4).reshape(num_rows, TOWERS, -1)
     stitch_out_grad = sog[:, :4].transpose(1, 0, 2).reshape(TOWERS, TOWERS, -1)
-    grad_mixed = gf.transpose(0, 2, 1, 3).astype(f32).reshape(num_rows, TOWERS, chans, -1)
-    grad_pooled, grad_si = pull_first(grad_mixed)
-    spread = jnp.einsum(
-        "rtcq,pq->rpct", grad_pooled * (1.0 / 9.0), pool_table(f32), precision=lax.Precision.HIGHEST
-    )
-    conv_grad = spread.reshape(num_rows, MAP * MAP, merged).astype(bf16)
-    stitch_in_grad = lax.psum(grad_si, "blk")
+    conv_grad, si, weight_grad = leave(s_rows, gf, pooled, weight_grad, conv_maps.shape[1])
+    conv_grad = conv_grad.transpose(1, 0, 2)
+    si = total_over_blk(si)
+    same, cross = si[0].reshape(chans, TOWERS), si[1].reshape(chans, TOWERS)
+    stitch_in_grad = jnp.stack(
+        [jnp.stack([same[:, 0], cross[:, 1]]), jnp.stack([cross[:, 0], same[:, 1]])])
     return (activations, conv_grad, weight_grad, bias_grad, stitch_in_grad, stitch_out_grad)
 
 

time: 375 us -> 232 us (0.62); the launches traced: 379 us -> 231 us
  local copies, waits for them, and re-layouts: 74.2 us -> 13.3 us
  blocking collectives: 55 us -> 0 us
  matrix products: 36.3 us -> 0 us
  Pallas kernels: 209 us -> 215 us
    psum x1 -> x0, blocking collectives: 36.5 us -> none  [body_ring(): stitch_in_grad = lax.psum(grad_si, 'blk')]
    dot_general x5 -> x0, matrix products: 36.3 us -> none  [the longest x3 25 us: stitch_first(): jnp.einsum('tuc,rucq->rtcq', stitch_in, pooled, precision=lax.Precision.H...]
    pallas_call x0 -> x3, Pallas kernels: none -> 32 us  [the longest x1 12.9 us: leave(): pl.pallas_call(exit_kernel, grid=(chunks,), out_shape=(jax.ShapeDtypeStru...]
    pallas_call x1, Pallas kernels: 209 us -> 183 us  [fc_layer(): pl.pallas_call(functools.partial(fc_kernel, steps), out_shape=(jax.ShapeD...]
    reshape x2 -> x3, local copies, waits for them, and re-layouts: 20.3 us -> 0.42 us  [the longest x1 0.14 us: body_ring(): back = jnp.stack([stitch_in[1, 0], stitch_in[0, 1]], 1).reshape(1, -1)]
    convert_element_type x2 -> x0, local copies, waits for them, and re-layouts: 17.8 us -> none  [the longest x1 13 us: body_ring(): conv_grad = spread.reshape(num_rows, MAP * MAP, merged).astype(bf16)]
    unnamed x18 -> x13, local copies, waits for them, and re-layouts: 20.9 us -> 5.58 us
    unnamed x1 -> x0, blocking collectives: 13.1 us -> none
where the time goes in v2:
time: 232 us; the launch traced here: 231 us
  Pallas kernels  215 us (93%)
  local copies, waits for them, and re-layouts  13.3 us (6%)
    pallas_call x1, Pallas kernels, fc_layer(): pl.pallas_call(functools.partial(fc_kernel, steps), out_shape=(jax.ShapeD...  183 us
    pallas_call x1, Pallas kernels, leave(): pl.pallas_call(exit_kernel, grid=(chunks,), out_shape=(jax.ShapeDtypeStru...  12.9 us
    pallas_call x1, Pallas kernels, entry(): pl.pallas_call(entry_kernel, grid=(chunks,), out_shape=(jax.ShapeDtypeStr...  12.5 us
    pallas_call x1, Pallas kernels, total_over_blk(): pl.pallas_call(total_kernel, out_shape=jax.ShapeDtypeStruct(value.shape,...  6.46 us
    unnamed x13, local copies, waits for them, and re-layouts  5.58 us

profile of v2, /device:TPU:0, one launch (start us, length us, event | category | flops | bytes accessed | tf_op | source)
XLA Modules:
  0.0 231.1 jit_solution(3920499889303809039)
XLA Ops:
  0.6 0.0 copy-start.5
  0.6 0.8 slice_bitcast_fusion.1
  1.4 0.1 copy.21
  1.5 0.1 reshape.31
  1.7 0.1 copy.22
  1.8 0.1 reshape.32
  1.9 0.1 copy.20
  2.0 0.1 reshape.30
  2.2 1.4 reshape.36
  3.5 0.1 copy.31
  3.7 0.0 copy-start
  3.7 2.6 %copy-done = bf16[128,169,128]{2,0,1:T(8,128)(2,1)S(1)} copy-done((bf16[128,169,128]{2,0,1:T(8,128)(2,1)S(1)}, bf16[128,169,128]{2,0,1:T(8,128)(2,1)}, u32[]{:S(2)}) %copy-start) | copy-done | bytes 5537816
  6.2 0.0 copy-start.1
  6.2 1.0 copy-done.1
  7.3 0.0 copy-start.3
  7.3 0.7 copy-done.3
  8.0 0.0 copy-start.4
  8.0 0.7 copy-done.4
  8.7 12.5 %shard_map.136 = (bf16[8,2,16,2304]{3,2,1,0:T(8,128)(2,1)}, f32[8,36,16,128]{3,2,1,0:T(8,128)S(1)}, s32[8,8,128]{2,1,0:T(8,128)S(1)}, f32[8,128]{1,0:T(8,128)S(1)}) custom-call(s32[32]{0:T(128)S(1)} %copy-done.4, f32[2,2,1024]{2,1,0:T(2,128)S(1)} %copy-done.3, f32[4,128]{1,0:T(4,128)S(1)} %pad_maximum_fusion.s_ref, bf16[512,512]{1,0:T(8,128)(2,1)S(1)} %copy-done.1, ...), custom_call_target="tpu_custom_call" | custom-call | flops 1073741824 | bytes 10485760 | tf_op jit(solution)/shard_map/pallas_call | solution.py:896
  21.2 0.2 slice_reduce_fusion.4
  21.4 0.6 fusion.1
  22.8 0.0 copy-done.5
  22.8 0.0 copy-start.2
  22.8 184.1 %conditional.1 = ((bf16[8,8,2,16,128]{4,3,2,1,0:T(8,128)(2,1)}, bf16[8,2,16,2304]{3,2,1,0:T(8,128)(2,1)}, f32[2,512,2304]{2,1,0:T(8,128)}, f32[2,512]{1,0:T(2,128)S(1)}, f32[8,8,128]{2,1,0:T(8,128)S(1)})) conditional(s32[]{:T(128)} %clamp.3, (s32[8]{0:T(128)S(1)}, f32[8,128]{1,0:T(8,128)S(1)}, f32[2,4096]{1,0:T(2,128)S(1)}, ...), branch_computations={%region_1.0_spmd, %region_2.0_spmd, %region_3.0_spmd} | conditional | flops 14495514624 | bytes 32505864 | solution.py:988
  22.8 0.9 copy.24.cot_ref
  23.7 183.0 %branch_0_fun.1 = (bf16[8,8,2,16,128]{4,3,2,1,0:T(8,128)(2,1)}, bf16[8,2,16,2304]{3,2,1,0:T(8,128)(2,1)}, f32[2,512,2304]{2,1,0:T(8,128)}, f32[2,512]{1,0:T(2,128)S(1)}, f32[8,8,128]{2,1,0:T(8,128)S(1)}) custom-call(s32[8]{0:T(128)S(1)} %get-tuple-element.36.n_ref, f32[8,128]{1,0:T(8,128)S(1)} %get-tuple-element.37.so_ref, ...), custom_call_target="tpu_custom_call" | custom-call | flops 9059696640 | bytes 31457280 | tf_op jit(solution)/shard_map/cond/branch_0_fun/pallas_call | solution.py:598
  206.9 1.4 copy.27
  208.3 0.9 reshape.34
  209.2 0.6 reshape.35
  209.8 0.0 copy-done.2
  209.8 12.9 %shard_map.137 = (bf16[169,128,128]{2,1,0:T(8,128)(2,1)}, f32[8,128]{1,0:T(8,128)S(1)}, f32[2,512,2304]{2,1,0:T(8,128)}) custom-call(f32[4,128]{1,0:T(4,128)S(1)} %pad_maximum_fusion.s_ref, bf16[512,512]{1,0:T(8,128)(2,1)S(1)} %copy-done.2, bf16[8,2,16,2304]{3,2,1,0:T(8,128)(2,1)} %get-tuple-element.76.gf_ref, ...), custom_call_target="tpu_custom_call" | custom-call | flops 1073741824 | bytes 31457280 | tf_op jit(solution)/shard_map/pallas_call | solution.py:929
  222.8 6.5 %shard_map.138 = f32[8,128]{1,0:T(8,128)S(1)} custom-call(f32[8,128]{1,0:T(8,128)S(1)} %get-tuple-element.82.x_ref), custom_call_target="tpu_custom_call" | custom-call | tf_op jit(solution)/shard_map/pallas_call | solution.py:954
  229.3 0.1 reshape_squeeze.7
  229.4 0.2 slice_reduce_fusion.2
  229.6 0.1 reshape_squeeze.6
  229.8 0.2 slice_reduce_fusion.3
  230.0 0.6 pad_maximum_fusion.1
  230.6 0.6 copy.48
  (7 shorter events, 0.1 us)
Async XLA Ops:
  0.6 22.1 %copy-start.5 = (f32[2,4096]{1,0:T(2,128)S(1)}, f32[2,4096]{1,0:T(2,128)}, u32[]{:S(2)}) copy-start(f32[2,4096]{1,0:T(2,128)} %param.15) | copy-start | bytes 98308
  3.7 2.6 %copy-start = (bf16[128,169,128]{2,0,1:T(8,128)(2,1)S(1)}, bf16[128,169,128]{2,0,1:T(8,128)(2,1)}, u32[]{:S(2)}) copy-start(bf16[128,169,128]{2,0,1:T(8,128)(2,1)} %param.12) | copy-start | bytes 16613380
  6.2 1.0 copy-start.1
  7.3 0.7 copy-start.3
  8.0 0.7 copy-start.4
  22.8 187.1 %copy-start.2 = (bf16[512,512]{1,0:T(8,128)(2,1)S(1)}, bf16[512,512]{1,0:T(8,128)(2,1)}, u32[]{:S(2)}) copy-start(bf16[512,512]{1,0:T(8,128)(2,1)} %constant.20.clone.perm_ref) | copy-start | bytes 1572868

commit v3 on v2

--- a/solution.py
+++ b/solution.py
@@ -12,7 +12,9 @@
 GRID = 6
 TOWERS = 2
 CHUNK = 16
-SPAN = 4
+SPAN = 2
+PIECES = 4
+HELD = 16
 PLACES = 8
 FEATS = 4
 RING_BLK = (0, 2, 4, 6, 7, 5, 3, 1)
@@ -112,27 +114,31 @@
 
 def fc_kernel(
     steps,
-    n_ref, so_ref, bias_ref, x_ref, cot_ref, w_hbm,
+    n_ref, so_ref, bias_ref, x_ref, cot_ref, relay_ref, w_hbm,
     act_out, gf_out, wg_hbm, bg_out, sog_out,
-    w, x, land, ring_tx, ex_tx, ex_rx, gp, part, sum_rx, held, sums,
-    cot_rx, acts, act_tx, act_rx, sog_acc, sog_tx, sog_rx, wg_tx,
+    w, x, land, ring_tx, ex_tx, ex_rx, gp, part, held, sums,
+    cot_rx, acts, act_tx, act_rx, sog_acc, sog_tx, sog_rx, wg_acc,
     kd, nn, start, tot, slot_rc, slot_live,
     w_sem, ag_ss, ag_rs, rs_ss, rs_rs, ex_ss, ex_rs, gp_ss, gp_rs,
-    cot_ss, cot_rs, act_ss, act_rs, sog_ss, sog_rs, wg_sem,
+    cot_ss, cot_rs, act_ss, act_rs, sog_ss, sog_rs, wg_sem, free,
 ):
     blk, feat = lax.axis_index("blk"), lax.axis_index("feat")
     place = ring_place(blk)
     ring_to = (ring_blk(lax.rem(place + 1, 8)), ring_blk(lax.rem(place + 7, 8)))
     ring_from = (lax.rem(place + 7, 8), lax.rem(place + 1, 8))
-    groups = x.shape[0] - 1
+    per = 2 * SPAN
+    groups = x.shape[0] - 8 // per
     slots = groups * SPAN
-    sent = 2 * (steps - 1)
-    feats_dim = x.shape[-1]
+    sent = PIECES * (steps - 1)
+    part_dim = x.shape[-1]
     units = w.shape[1]
     quarter = units // FEATS
     row_feat = lax.div(blk, 2)
     half_at = lax.rem(blk, 2) * FEATS + feat
     mine = row_feat == feat
+    side = 2 * lax.div(feat, 2)
+    cot_feat = side + lax.rem(row_feat, 2)
+    cot_mine = cot_feat == feat
 
     w_copy = pltpu.make_async_copy(w_hbm, w, w_sem)
     w_copy.start()
@@ -147,6 +153,14 @@
     for o in range(1, FEATS):
         hello((blk, lax.rem(feat + o, FEATS)))
 
+    def cot_to(s):
+        owner = lax.rem(feat + 2 * lax.div(s, 4), FEATS)
+        return 2 * owner + lax.rem(lax.div(s, 2), 2), side + lax.rem(s, 2)
+
+    def cot_not_me(s):
+        to = cot_to(s)
+        return jnp.logical_or(to[0] != blk, to[1] != feat)
+
     def hello_far(s, carry):
         to = (2 * feat + lax.div(s, FEATS), lax.rem(s, FEATS))
 
@@ -158,21 +172,32 @@
         def _():
             hello((s, row_feat))
 
+        @pl.when(cot_not_me(s))
+        def _():
+            hello(cot_to(s))
+
+        @pl.when(jnp.logical_or(s != blk, cot_feat != feat))
+        def _():
+            hello((s, cot_feat))
+
         return carry
 
     lax.fori_loop(0, 8, hello_far, 0)
-    pl.semaphore_wait(bar, jnp.where(mine, 2 + 3 + 14, 2 + 3 + 16))
-
-    def cot_copy(s):
-        return pltpu.make_async_remote_copy(
-            src_ref=cot_ref.at[s], dst_ref=cot_rx.at[blk], send_sem=cot_ss.at[s],
-            recv_sem=cot_rs.at[blk],
-            device_id=(2 * feat + lax.div(s, FEATS), lax.rem(s, FEATS)), device_id_type=MESH)
+    pl.semaphore_wait(
+        bar, jnp.where(mine, 2 + 3 + 14, 2 + 3 + 16) + jnp.where(cot_mine, 14, 16))
+
+    def own_cot(s):
+        return lax.div(s, 2) * FEATS + side + lax.rem(s, 2)
+
+    def cot_copy(s, src):
+        return pltpu.make_async_remote_copy(
+            src_ref=src, dst_ref=cot_rx.at[blk], send_sem=cot_ss.at[s],
+            recv_sem=cot_rs.at[blk], device_id=cot_to(s), device_id_type=MESH)
 
     def cot_wait(r):
         return pltpu.make_async_remote_copy(
             src_ref=cot_ref.at[0], dst_ref=cot_rx.at[r], send_sem=cot_ss.at[0],
-            recv_sem=cot_rs.at[r], device_id=(r, row_feat), device_id_type=MESH)
+            recv_sem=cot_rs.at[r], device_id=(r, cot_feat), device_id_type=MESH)
 
     def far_not_me(s):
         return jnp.logical_or(2 * feat + lax.div(s, FEATS) != blk, lax.rem(s, FEATS) != feat)
@@ -182,7 +207,9 @@
 
     for c in range(8):
         for t in range(TOWERS):
-            x[groups, t, c // SPAN, c % SPAN] = x_ref[c, t]
+            for h in range(2):
+                x[groups + c // per, t, h, c % per // SPAN, c % SPAN] = x_ref[
+                    c, t, :, h * part_dim:(h + 1) * part_dim]
 
     run = jnp.int32(0)
     for q in range(PLACES):
@@ -196,31 +223,42 @@
 
     def ring_unit_copy(d, m):
         return pltpu.make_async_remote_copy(
-            src_ref=ring_tx.at[d, lax.rem(m, 4)], dst_ref=land.at[d, m],
-            send_sem=ag_ss.at[d, lax.rem(m, 4)], recv_sem=ag_rs.at[d, m],
+            src_ref=ring_tx.at[d, lax.rem(m, 8)], dst_ref=land.at[d, m],
+            send_sem=ag_ss.at[d, lax.rem(m, 8)], recv_sem=ag_rs.at[d, m],
             device_id=(ring_to[d], feat), device_id_type=MESH)
 
     own_k = (kd[place], kd[PLACES + place])
     prev_k = tuple(kd[d * PLACES + ring_from[d]] for d in (0, 1))
     own_base = (0, own_k[0])
-    for m in (0, 1):
+
+    def own_piece(c, t, h):
+        return x[groups + lax.div(c, per), t, h, lax.div(lax.rem(c, per), SPAN), lax.rem(c, SPAN)]
+
+    for m in range(PIECES):
         for d in (0, 1):
-            c = own_base[d]
-            ring_tx[d, m] = x[groups, m, lax.div(c, SPAN), lax.rem(c, SPAN)] if d else x[groups, m, 0, 0]
+            ring_tx[d, m] = own_piece(jnp.int32(own_base[d]), m // 2, m % 2)
             ring_unit_copy(d, jnp.int32(m)).start()
 
     def cot_send(s, carry):
-        @pl.when(far_not_me(s))
-        def _():
-            cot_copy(s).start()
-
-        @pl.when(jnp.logical_not(far_not_me(s)))
-        def _():
-            cot_rx[blk] = cot_ref[s]
+        @pl.when(cot_not_me(s))
+        def _():
+            cot_copy(s, cot_ref.at[own_cot(s)]).start()
+
+        @pl.when(jnp.logical_not(cot_not_me(s)))
+        def _():
+            cot_rx[blk] = cot_ref[own_cot(s)]
+
+        @pl.when(cot_not_me(s + 4))
+        def _():
+            cot_copy(s + 4, relay_ref.at[s]).start()
+
+        @pl.when(jnp.logical_not(cot_not_me(s + 4)))
+        def _():
+            cot_rx[blk] = relay_ref[s]
 
         return carry
 
-    lax.fori_loop(0, 8, cot_send, 0)
+    lax.fori_loop(0, 4, cot_send, 0)
 
     for d in (0, 1):
         run = jnp.int32(0)
@@ -246,7 +284,6 @@
     own_at = (tot[0] - own_k[0], tot[1] - own_k[1])
     held[...] = jnp.zeros_like(held)
     sog_acc[...] = jnp.zeros_like(sog_acc)
-    w_copy.wait()
 
     def ex_copy(slot, g, o):
         to = lax.rem(feat + o, FEATS)
@@ -281,14 +318,16 @@
                 ex_copy(slot, g, o).wait_send()
 
         for t in range(TOWERS):
-            rows = x[g, t].reshape(2 * SPAN * CHUNK, feats_dim)
-            for h in range(2):
-                out = lax.dot_general(
-                    rows, w[t, 2 * h * quarter:2 * (h + 1) * quarter],
-                    (((1,), (1,)), ((), ())), preferred_element_type=f32)
+            for n in range(2):
+                out = sum(
+                    lax.dot_general(
+                        x[g, t, h].reshape(per * CHUNK, part_dim),
+                        w[t, 2 * n * quarter:2 * (n + 1) * quarter, h * part_dim:(h + 1) * part_dim],
+                        (((1,), (1,)), ((), ())), preferred_element_type=f32)
+                    for h in range(2))
                 for e in range(2):
-                    ex_tx[slot, 2 * h + e, t] = out[:, e * quarter:(e + 1) * quarter].reshape(
-                        2 * SPAN, CHUNK, quarter)
+                    ex_tx[slot, 2 * n + e, t] = out[:, e * quarter:(e + 1) * quarter].reshape(
+                        per, CHUNK, quarter)
         for o in range(1, FEATS):
             ex_copy(slot, g, o).start()
         ex_rx[g, feat] = ex_tx[slot, feat]
@@ -329,101 +368,102 @@
                 gp[g, feat, u, s] = (slope[u] * back).astype(bf16)
             return carry
 
-        lax.fori_loop(0, 2 * SPAN, one, 0)
+        lax.fori_loop(0, per, one, 0)
         for o in range(1, FEATS):
             gp_copy(g, o).start()
 
-    tile = feats_dim // 3
+    tile = part_dim // 3
 
     def backward(g):
         for o in range(1, FEATS):
             gp_wait(g, o).wait_recv()
         for t in range(TOWERS):
             rows = jnp.concatenate(
-                [gp[g, q, t].reshape(2 * SPAN * CHUNK, quarter) for q in range(FEATS)], axis=1)
-            for n in range(3):
-                part[t, :, :, n * tile:(n + 1) * tile] = jnp.dot(
-                    rows, w[t, :, n * tile:(n + 1) * tile],
-                    preferred_element_type=f32).reshape(2 * SPAN, CHUNK, tile)
-
-    wide = feats_dim // 6
+                [gp[g, q, t].reshape(per * CHUNK, quarter) for q in range(FEATS)], axis=1)
+            for h in range(2):
+                part[t, h] = jnp.dot(
+                    rows, w[t, :, h * part_dim:(h + 1) * part_dim],
+                    preferred_element_type=f32).reshape(per, CHUNK, part_dim)
+
+    def tile_at(q):
+        t, n = lax.div(q, 6), lax.rem(q, 6)
+        return t, lax.div(n, 3), pl.multiple_of(n * tile, 128), pl.multiple_of(lax.rem(n, 3) * tile, 128)
 
     def wg_copy(q):
-        return pltpu.make_async_copy(
-            wg_tx.at[lax.rem(q, 2)],
-            wg_hbm.at[lax.div(q, 6), :, pl.ds(pl.multiple_of(lax.rem(q, 6) * wide, 128), wide)],
-            wg_sem.at[lax.rem(q, 2)])
-
-    def weight_tile(q):
-        t = lax.div(q, 6)
-        cols = pl.ds(pl.multiple_of(lax.rem(q, 6) * wide, 128), wide)
-
-        @pl.when(q >= 2)
-        def _():
-            wg_copy(q).wait()
-
-        rows = x[0:groups, t, :, :, :, cols].reshape(groups * 2 * SPAN * CHUNK, wide)
+        t, _, whole_at, _ = tile_at(q)
+        cols = pl.ds(whole_at, tile)
+        return pltpu.make_async_copy(wg_acc.at[t, :, cols], wg_hbm.at[t, :, cols], wg_sem.at[q])
+
+    def weight_tile(q, first, count):
+        t, h, whole_at, part_at = tile_at(q)
+        rows = x[first:first + count, t, h, :, :, :, pl.ds(part_at, tile)].reshape(
+            count * per * CHUNK, tile)
         for e in range(FEATS):
-            grads = gp[0:groups, e, t].reshape(groups * 2 * SPAN * CHUNK, quarter)
-            wg_tx[lax.rem(q, 2), e * quarter:(e + 1) * quarter] = lax.dot_general(
+            grads = gp[first:first + count, e, t].reshape(count * per * CHUNK, quarter)
+            value = lax.dot_general(
                 grads, rows, (((0,), (0,)), ((), ())), preferred_element_type=f32)
-        wg_copy(q).start()
+            at = (t, pl.ds(e * quarter, quarter), pl.ds(whole_at, tile))
+            wg_acc[at] = value + wg_acc[at] if first else value
 
     def gather_unit(g, q):
-        u = 2 * SPAN * g + q
-        ci, t = lax.div(q, 2), lax.rem(q, 2)
+        u = PIECES * SPAN * g + q
+        ci, t, h = lax.div(q, PIECES), lax.rem(lax.div(q, 2), 2), lax.rem(q, 2)
         i = SPAN * g + ci
         for d in (0, 1):
-            c = jnp.clip(i - own_at[d], 0, own_k[d] - 1) + own_base[d]
-            own = x[groups, t, lax.div(c, SPAN), lax.rem(c, SPAN)]
+            own = own_piece(jnp.clip(i - own_at[d], 0, own_k[d] - 1) + own_base[d], t, h)
 
             @pl.when(u < sent)
             def _(d=d, own=own):
                 ring_unit_copy(d, u).wait_recv()
-                x[g, t, d, ci] = jnp.where(i >= own_at[d], own, land[d, u])
+                x[g, t, h, d, ci] = jnp.where(i >= own_at[d], own, land[d, u])
 
             @pl.when(u >= sent)
             def _(d=d, own=own):
-                x[g, t, d, ci] = own
-
-        m = u + 2
-        for d in (0, 1):
+                x[g, t, h, d, ci] = own
+
+            m = u + PIECES
+
             @pl.when(m < sent)
             def _(d=d):
-                @pl.when(m >= 4)
+                @pl.when(m >= 8)
                 def _():
                     ring_unit_copy(d, m).wait_send()
 
-                im = i + 1
-                here = im < own_k[d]
-                cm = jnp.minimum(im, own_k[d] - 1) + own_base[d]
-                src = jnp.maximum(im - own_k[d], 0)
-                ring_tx[d, lax.rem(m, 4)] = x[
-                    jnp.where(here, groups, lax.div(src, SPAN)), t,
-                    jnp.where(here, lax.div(cm, SPAN), d),
-                    jnp.where(here, lax.rem(cm, SPAN), lax.rem(src, SPAN))]
+                here = i + 1 < own_k[d]
+                c = jnp.minimum(i + 1, own_k[d] - 1) + own_base[d]
+                src = jnp.maximum(i + 1 - own_k[d], 0)
+                ring_tx[d, lax.rem(m, 8)] = x[
+                    jnp.where(here, groups + lax.div(c, per), lax.div(src, SPAN)), t, h,
+                    jnp.where(here, lax.div(lax.rem(c, per), SPAN), d),
+                    jnp.where(here, lax.rem(c, SPAN), lax.rem(src, SPAN))]
                 ring_unit_copy(d, m).start()
 
     def sum_copy(d, v):
         return pltpu.make_async_remote_copy(
-            src_ref=sums.at[d, v], dst_ref=sum_rx.at[d, v], send_sem=rs_ss.at[d, v],
+            src_ref=sums.at[d, v], dst_ref=land.at[d, v], send_sem=rs_ss.at[d, lax.rem(v, HELD)],
             recv_sem=rs_rs.at[d, v], device_id=(ring_to[d], feat), device_id_type=MESH)
 
     def sum_unit(g, q):
-        v = 2 * SPAN * g + q
-        ci, t = lax.div(q, 2), lax.rem(q, 2)
+        v = PIECES * SPAN * g + q
+        ci, t, h = lax.div(q, PIECES), lax.rem(lax.div(q, 2), 2), lax.rem(q, 2)
+        before = v - PIECES
         for d in (0, 1):
-            @pl.when(jnp.logical_and(v >= 2, v - 2 < sent))
+            @pl.when(jnp.logical_and(before >= 0, before < sent))
             def _(d=d):
-                sum_copy(d, v - 2).wait_recv()
-                held[d, lax.rem(v - 2, 8)] = sum_rx[d, v - 2]
-
-            came = held[d, lax.rem(v - 2 * prev_k[d] + 8, 8)].astype(f32)
-            value = part[t, d * SPAN + ci] + came * jnp.where(v >= 2 * prev_k[d], f32(1), f32(0))
+                sum_copy(d, before).wait_recv()
+                held[d, lax.rem(before, HELD)] = land[d, before]
+
+            came = held[d, lax.rem(v - PIECES * prev_k[d] + HELD, HELD)].astype(f32)
+            value = part[t, h, d * SPAN + ci] + came * jnp.where(
+                v >= PIECES * prev_k[d], f32(1), f32(0))
             sums[d, v] = value.astype(bf16)
 
             @pl.when(v < sent)
             def _(d=d):
+                @pl.when(v >= HELD)
+                def _():
+                    sum_copy(d, v).wait_send()
+
                 sum_copy(d, v).start()
 
     def act_copy(r):
@@ -478,15 +518,35 @@
 
         lax.fori_loop(0, PLACES, send, 0)
 
+    def add_bias():
+        for e in range(FEATS):
+            for t in range(TOWERS):
+                def add(g, total, e=e, t=t):
+                    return total + jnp.sum(gp[g, e, t].astype(f32), axis=0)
+
+                total = lax.fori_loop(0, groups, add, jnp.zeros((CHUNK, quarter), f32))
+                bg_out[t:t + 1, e * quarter:(e + 1) * quarter] = jnp.sum(
+                    total, axis=0, keepdims=True)
+
+    early = groups - 2
+
     def iteration(it, carry):
         @pl.when(it >= 3)
         def _():
             backward(it - 3)
 
+        @pl.when(it == groups + 2)
+        def _():
+            add_bias()
+
+        @pl.when(it == 1)
+        def _():
+            w_copy.wait()
+
         @pl.when(it == 2)
         def _():
             def arrived(r, carry):
-                @pl.when(near_not_me(r))
+                @pl.when(jnp.logical_or(r != blk, cot_feat != feat))
                 def _():
                     cot_wait(r).wait_recv()
 
@@ -505,6 +565,11 @@
         @pl.when(it == groups + 1)
         def _():
             send_acts()
+
+        @pl.when(it >= 3)
+        def _():
+            for d in (0, 1):
+                pl.semaphore_wait(free.at[d], 1)
 
         def unit(q, carry):
             @pl.when(it < groups)
@@ -515,14 +580,30 @@
             def _():
                 sum_unit(it - 3, q)
 
+            @pl.when(jnp.logical_and(it == groups, q < 6))
+            def _():
+                weight_tile(q, 0, early)
+
+            @pl.when(jnp.logical_and(it == groups + 1, q < 6))
+            def _():
+                weight_tile(q + 6, 0, early)
+
             @pl.when(jnp.logical_and(it == groups + 2, q < 6))
             def _():
-                weight_tile(2 * q)
-                weight_tile(2 * q + 1)
+                for e in range(2):
+                    weight_tile(2 * q + e, early, 2)
+                    wg_copy(2 * q + e).start()
 
             return carry
 
-        lax.fori_loop(0, 2 * SPAN, unit, 0)
+        lax.fori_loop(0, PIECES * SPAN, unit, 0)
+
+        @pl.when(it < groups)
+        def _():
+            for d in (0, 1):
+                pl.semaphore_signal(
+                    free.at[d], inc=1, device_id=(ring_blk(ring_from[d]), feat), device_id_type=MESH)
+
         return carry
 
     lax.fori_loop(0, groups + 3, iteration, 0)
@@ -533,22 +614,19 @@
         i = jnp.clip(i, 0, slots - 1)
         keep = jnp.where(c < own_k[0] + own_k[1], f32(1), f32(0))
         for t in range(TOWERS):
-            gf_out[c, t] = (sums[d, 2 * i + t].astype(f32) * keep).astype(bf16)
-
-    for e in range(FEATS):
-        for t in range(TOWERS):
-            def add(g, total, e=e, t=t):
-                return total + jnp.sum(gp[g, e, t].astype(f32), axis=0)
-
-            total = lax.fori_loop(0, groups, add, jnp.zeros((CHUNK, quarter), f32))
-            bg_out[t:t + 1, e * quarter:(e + 1) * quarter] = jnp.sum(total, axis=0, keepdims=True)
+            for h in range(2):
+                gf_out[c, t, :, h * part_dim:(h + 1) * part_dim] = (
+                    sums[d, PIECES * i + 2 * t + h].astype(f32) * keep).astype(bf16)
 
     def finish(s, carry):
         @pl.when(far_not_me(s))
         def _():
             act_wait(s).wait_recv()
             sog_wait(s).wait_recv()
-            cot_copy(s).wait_send()
+
+        @pl.when(cot_not_me(s))
+        def _():
+            cot_copy(s, cot_ref.at[0]).wait_send()
 
         @pl.when(near_not_me(s))
         def _():
@@ -566,8 +644,8 @@
             sum_copy(d, v).wait_send()
         return carry
 
-    lax.fori_loop(0, sent, finish_sums, 0)
-    for m in range(sent - 4, sent):
+    lax.fori_loop(sent - HELD, sent, finish_sums, 0)
+    for m in range(sent - 8, sent):
         for d in (0, 1):
             ring_unit_copy(d, jnp.int32(m)).wait_send()
     for o in range(1, FEATS):
@@ -579,11 +657,11 @@
             return carry
 
         lax.fori_loop(0, groups, finish_gp, 0)
-    for q in (10, 11):
+    for q in range(12):
         wg_copy(jnp.int32(q)).wait()
 
 
-def fc_layer(steps, number, n, so, bias, x, cot, weight):
+def fc_layer(steps, number, n, so, bias, x, cot, relay, weight):
     units, feats_dim = weight.shape[1:]
     quarter = units // FEATS
     groups = -(-steps // SPAN)
@@ -591,7 +669,7 @@
     vm = pltpu.VMEM
     dma = pltpu.SemaphoreType.DMA
     sm = pltpu.SMEM
-    unit = (CHUNK, feats_dim)
+    unit = (CHUNK, feats_dim // 2)
     vmem_spec = pl.BlockSpec(memory_space=pltpu.VMEM)
     any_spec = pl.BlockSpec(memory_space=pl.ANY)
     rows = 2 * slots * CHUNK
@@ -599,25 +677,24 @@
         functools.partial(fc_kernel, steps),
         out_shape=(
             jax.ShapeDtypeStruct((8, 8, TOWERS, CHUNK, quarter), bf16),
-            jax.ShapeDtypeStruct((8, TOWERS) + unit, bf16),
+            jax.ShapeDtypeStruct((8, TOWERS, CHUNK, feats_dim), bf16),
             jax.ShapeDtypeStruct(weight.shape, f32),
             jax.ShapeDtypeStruct((TOWERS, units), f32),
             jax.ShapeDtypeStruct((8, 8, quarter), f32),
         ),
-        in_specs=[pl.BlockSpec(memory_space=pltpu.SMEM)] + [vmem_spec] * 4 + [any_spec],
+        in_specs=[pl.BlockSpec(memory_space=pltpu.SMEM)] + [vmem_spec] * 5 + [any_spec],
         out_specs=(vmem_spec, vmem_spec, any_spec, vmem_spec, vmem_spec),
         scratch_shapes=[
             vm(weight.shape, bf16),
-            vm((groups + 1, TOWERS, 2, SPAN) + unit, bf16),
-            vm((2, 2 * steps - 2) + unit, bf16),
-            vm((2, 4) + unit, bf16),
+            vm((groups + 8 // (2 * SPAN), TOWERS, 2, 2, SPAN) + unit, bf16),
+            vm((2, PIECES * (steps - 1)) + unit, bf16),
+            vm((2, 8) + unit, bf16),
             vm((2, FEATS, TOWERS, 2 * SPAN, CHUNK, quarter), f32),
             vm((groups, FEATS, TOWERS, 2 * SPAN, CHUNK, quarter), f32),
             vm((groups, FEATS, TOWERS, 2 * SPAN, CHUNK, quarter), bf16),
-            vm((TOWERS, 2 * SPAN) + unit, f32),
-            vm((2, 2 * steps - 2) + unit, bf16),
-            vm((2, 8) + unit, bf16),
-            vm((2, 2 * slots) + unit, bf16),
+            vm((TOWERS, 2, 2 * SPAN) + unit, f32),
+            vm((2, HELD) + unit, bf16),
+            vm((2, PIECES * slots) + unit, bf16),
             vm((8, 8, TOWERS, CHUNK, quarter), bf16),
             vm((slots, 2, TOWERS, CHUNK, quarter), bf16),
             vm((8, 8, TOWERS, CHUNK, quarter), bf16),
@@ -625,7 +702,7 @@
             vm((4, CHUNK, quarter), f32),
             vm((8, quarter), f32),
             vm((8, 8, quarter), f32),
-            vm((2, units, feats_dim // 6), f32),
+            vm(weight.shape, f32),
             sm((2 * PLACES,), i32),
             sm((PLACES,), i32),
             sm((2 * PLACES,), i32),
@@ -633,10 +710,10 @@
             sm((2 * slots,), i32),
             sm((2 * slots,), i32),
             dma,
-            dma((2, 4)),
-            dma((2, 2 * steps - 2)),
-            dma((2, 2 * steps - 2)),
-            dma((2, 2 * steps - 2)),
+            dma((2, 8)),
+            dma((2, PIECES * (steps - 1))),
+            dma((2, HELD)),
+            dma((2, PIECES * (steps - 1))),
             dma((2, 3)),
             dma((groups, FEATS)),
             dma((groups, 3)),
@@ -647,14 +724,15 @@
             dma((8,)),
             dma((8,)),
             dma((8,)),
-            dma((2,)),
+            dma((12,)),
+            pltpu.SemaphoreType.REGULAR((2,)),
         ],
         cost_estimate=pl.CostEstimate(
             flops=6 * rows * TOWERS * units * feats_dim, bytes_accessed=30 << 20,
             transcendentals=rows * TOWERS * quarter),
         compiler_params=pltpu.CompilerParams(
             collective_id=number, has_side_effects=True, vmem_limit_bytes=60 << 20),
-    )(n, so, bias, x, cot, weight)
+    )(n, so, bias, x, cot, relay, weight)
 
 
 def layout_matrix(chans):
@@ -675,9 +753,9 @@
 
 
 def entry_kernel(
-    cc_ref, so_ref, s_ref, perm_ref, conv_ref,
-    feats_out, pooled_out, n_out, so_out,
-    n_tx, n_rx, so_tx, so_rx, n_ss, n_rs, so_ss, so_rs,
+    cc_ref, so_ref, s_ref, perm_ref, cot_ref, conv_ref,
+    feats_out, pooled_out, n_out, so_out, relay_out,
+    n_tx, n_rx, so_tx, so_rx, relay_rx, n_ss, n_rs, so_ss, so_rs, relay_ss, relay_rs,
 ):
     blk, feat = lax.axis_index("blk"), lax.axis_index("feat")
     step = pl.program_id(0)
@@ -700,6 +778,14 @@
         return pltpu.make_async_remote_copy(
             src_ref=so_tx.at[to], dst_ref=so_rx, send_sem=so_ss.at[o - 1], recv_sem=so_rs,
             device_id=(blk, to), device_id_type=MESH)
+
+    across_y = lax.rem(feat + 2, FEATS)
+
+    def relay_copy(s):
+        return pltpu.make_async_remote_copy(
+            src_ref=cot_ref.at[s // 2 * FEATS + 2 * lax.div(across_y, 2) + s % 2],
+            dst_ref=relay_rx.at[s], send_sem=relay_ss.at[s], recv_sem=relay_rs.at[s],
+            device_id=(blk, across_y), device_id_type=MESH)
 
     @pl.when(step == 0)
     def _():
@@ -723,6 +809,8 @@
         pl.semaphore_wait(bar, PLACES - 1 + FEATS - 1)
         for o in range(1, PLACES):
             n_copy(o).start()
+        for s in range(4):
+            relay_copy(s).start()
 
         @pl.when(holds)
         def _():
@@ -777,8 +865,11 @@
         def _():
             so_copy(1).wait_recv()
 
+        for s in range(4):
+            relay_copy(s).wait()
         n_out[...] = n_rx[...]
         so_out[...] = so_rx[...]
+        relay_out[...] = relay_rx[...]
 
 
 def exit_kernel(
@@ -886,7 +977,7 @@
         copy(o).wait_send()
 
 
-def entry(counts, so, s_rows, conv):
+def entry(counts, so, s_rows, cot, conv):
     spots, rows, merged = conv.shape
     chunks = rows // CHUNK
     chans = merged // TOWERS
@@ -901,22 +992,24 @@
             jax.ShapeDtypeStruct((chunks, GRID * GRID, CHUNK, merged), f32),
             jax.ShapeDtypeStruct((PLACES, 8, 128), i32),
             jax.ShapeDtypeStruct((8, 128), f32),
+            jax.ShapeDtypeStruct((4,) + cot.shape[1:], bf16),
         ),
-        in_specs=[pl.BlockSpec(memory_space=pltpu.SMEM)] + [whole] * 3 + [
+        in_specs=[pl.BlockSpec(memory_space=pltpu.SMEM)] + [whole] * 4 + [
             pl.BlockSpec((spots, CHUNK, merged), lambda c: (0, c, 0))],
         out_specs=(
             pl.BlockSpec((1, TOWERS, CHUNK, wide), lambda c: (c, 0, 0, 0)),
             pl.BlockSpec((1, GRID * GRID, CHUNK, merged), lambda c: (c, 0, 0, 0)),
-            whole, whole,
+            whole, whole, whole,
         ),
         scratch_shapes=[
             vm((8, 128), i32), vm((PLACES, 8, 128), i32), vm((FEATS, 8, 128), f32), vm((8, 128), f32),
-            dma((PLACES - 1,)), dma((PLACES,)), dma((FEATS - 1,)), dma,
+            vm((4,) + cot.shape[1:], bf16),
+            dma((PLACES - 1,)), dma((PLACES,)), dma((FEATS - 1,)), dma, dma((4,)), dma((4,)),
         ],
         cost_estimate=pl.CostEstimate(flops=1 << 30, bytes_accessed=10 << 20, transcendentals=0),
         compiler_params=pltpu.CompilerParams(
-            collective_id=8, has_side_effects=True, vmem_limit_bytes=40 << 20),
-    )(counts, so, s_rows, jnp.asarray(layout_matrix(chans), bf16), conv)
+            collective_id=20, has_side_effects=True, vmem_limit_bytes=60 << 20),
+    )(counts, so, s_rows, jnp.asarray(layout_matrix(chans), bf16), cot, conv)
 
 
 def leave(s_rows, gf, pooled, weight_grad, spots):
@@ -944,7 +1037,7 @@
         ),
         scratch_shapes=[vm((2, CHUNK, 128), f32)],
         cost_estimate=pl.CostEstimate(flops=1 << 30, bytes_accessed=30 << 20, transcendentals=0),
-        compiler_params=pltpu.CompilerParams(vmem_limit_bytes=40 << 20),
+        compiler_params=pltpu.CompilerParams(vmem_limit_bytes=60 << 20),
     )(s_rows, jnp.asarray(layout_matrix(merged // TOWERS), bf16), gf, pooled, weight_grad)
 
 
@@ -959,11 +1052,11 @@
         scratch_shapes=[
             pltpu.VMEM((PLACES,) + value.shape, f32), dma((PLACES - 1,)), dma((PLACES,))],
         compiler_params=pltpu.CompilerParams(
-            collective_id=9, has_side_effects=True, vmem_limit_bytes=16 << 20),
+            collective_id=21, has_side_effects=True, vmem_limit_bytes=16 << 20),
     )(value)
 
 
-CLASSES = (20, 24)
+CLASSES = (19, 20, 21, 22, 24)
 
 
 def body_ring(conv_maps, crop_counts, fc_weight, fc_bias, stitch_in, stitch_out, cotangent):
@@ -977,10 +1070,10 @@
     other = jnp.stack([stitch_in[0, 1], stitch_in[1, 0]], 1).reshape(1, -1)
     back = jnp.stack([stitch_in[1, 0], stitch_in[0, 1]], 1).reshape(1, -1)
     s_rows = jnp.concatenate([own, other, back, own], 0)
-    feats, pooled, counts, so = entry(
-        crop_counts, stitch_out, s_rows, conv_maps.transpose(1, 0, 2))
+    cot = cotangent.reshape(chunks, CHUNK, TOWERS, 8, quarter).transpose(3, 0, 2, 1, 4)
+    feats, pooled, counts, so, relay = entry(
+        crop_counts, stitch_out, s_rows, cot, conv_maps.transpose(1, 0, 2))
     n = counts[:, 0, 0]
-    cot = cotangent.reshape(chunks, CHUNK, TOWERS, 8, quarter).transpose(3, 0, 2, 1, 4)
     need = lax.div(jnp.sum(lax.div(n + (CHUNK - 1), CHUNK)) + 1, 2)
     full = PLACES * chunks // 2
     kinds = CLASSES + (full,)
@@ -988,7 +1081,7 @@
     act, gf, weight_grad, bias_grad, sog = lax.switch(
         pick,
         [functools.partial(fc_layer, steps, at) for at, steps in enumerate(kinds)],
-        n, so, fc_bias, feats, cot, fc_weight)
+        n, so, fc_bias, feats, cot, relay, fc_weight)
     activations = act.transpose(1, 3, 2, 0, 4).reshape(num_rows, TOWERS, -1)
     stitch_out_grad = sog[:, :4].transpose(1, 0, 2).reshape(TOWERS, TOWERS, -1)
     conv_grad, si, weight_grad = leave(s_rows, gf, pooled, weight_grad, conv_maps.shape[1])

time: 232 us -> 210 us (0.905)
  Pallas kernels: 215 us -> 198 us
  local copies, waits for them, and re-layouts: 13.3 us -> 7.79 us
    pallas_call x1, Pallas kernels: 183 us -> 162 us  [fc_layer(): pl.pallas_call(functools.partial(fc_kernel, steps), out_shape=(jax.ShapeD...]
    unnamed x13 -> x5, local copies, waits for them, and re-layouts: 5.58 us -> 1.28 us
    pallas_call x1, Pallas kernels: 12.5 us -> 16 us  [entry(): pl.pallas_call(entry_kernel, grid=(chunks,), out_shape=(jax.ShapeDtypeStr...]
where the time goes in v3:
time: 210 us
  Pallas kernels  198 us (94%)
  local copies, waits for them, and re-layouts  7.79 us (4%)
    pallas_call x1, Pallas kernels, fc_layer(): pl.pallas_call(functools.partial(fc_kernel, steps), out_shape=(jax.ShapeD...  162 us
    pallas_call x1, Pallas kernels, entry(): pl.pallas_call(entry_kernel, grid=(chunks,), out_shape=(jax.ShapeDtypeStr...  16 us
    pallas_call x1, Pallas kernels, leave(): pl.pallas_call(exit_kernel, grid=(chunks,), out_shape=(jax.ShapeDtypeStru...  13.3 us
    pallas_call x1, Pallas kernels, total_over_blk(): pl.pallas_call(total_kernel, out_shape=jax.ShapeDtypeStruct(value.shape,...  6.46 us

profile of v3, /device:TPU:0, one launch (start us, length us, event | category | flops | bytes accessed | tf_op | source)
XLA Modules:
  0.0 209.6 jit_solution(16841251396371915918)
XLA Ops:
  0.6 0.0 copy-start.1
  0.6 0.8 slice_bitcast_fusion.1
  1.4 0.1 copy.21
  1.5 0.1 reshape.31
  1.7 0.1 copy.22
  1.8 0.1 reshape.32
  1.9 0.1 copy.20
  2.0 0.1 reshape.30
  2.1 0.6 pad_maximum_fusion.s_ref
  2.7 1.4 reshape.36
  4.1 0.1 copy.30
  4.2 16.0 %shard_map.136 = (bf16[8,2,16,2304]{3,2,1,0:T(8,128)(2,1)S(1)}, f32[8,36,16,128]{3,2,1,0:T(8,128)}, s32[8,8,128]{2,1,0:T(8,128)}, f32[8,128]{1,0:T(8,128)S(1)}, bf16[4,8,2,16,128]{4,3,2,1,0:T(8,128)(2,1)}) custom-call(s32[32]{0:T(128)} %cc_ref.1, f32[2,2,1024]{2,1,0:T(2,128)} %so_ref.1, f32[4,128]{1,0:T(4,128)} %pad_maximum_fusion.s_ref, ...), custom_call_target="tpu_custom_call" | custom-call | flops 1073741824 | bytes 10485760 | tf_op jit(solution)/shard_map/pallas_call | solution.py:987
  20.2 1.0 slice_reduce_fusion.4
  21.2 0.6 fusion.1
  22.6 0.0 copy-done.1
  22.6 162.7 %conditional.1 = ((bf16[8,8,2,16,128]{4,3,2,1,0:T(8,128)(2,1)S(1)}, bf16[8,2,16,2304]{3,2,1,0:T(8,128)(2,1)S(1)}, f32[2,512,2304]{2,1,0:T(8,128)}, f32[2,512]{1,0:T(2,128)S(1)}, f32[8,8,128]{2,1,0:T(8,128)S(1)})) conditional(s32[]{:T(128)} %clamp.3, (s32[8]{0:T(128)S(1)}, f32[8,128]{1,0:T(8,128)S(1)}, ...), branch_computations={%region_1.0_spmd, %region_2.0_spmd, %region_3.0_spmd, %region_4.0_... | conditional | flops 14495514624 | bytes 31457288 | solution.py:1081
  22.8 162.0 %branch_1_fun.1 = (bf16[8,8,2,16,128]{4,3,2,1,0:T(8,128)(2,1)S(1)}, bf16[8,2,16,2304]{3,2,1,0:T(8,128)(2,1)S(1)}, f32[2,512,2304]{2,1,0:T(8,128)}, f32[2,512]{1,0:T(2,128)S(1)}, f32[8,8,128]{2,1,0:T(8,128)S(1)}) custom-call(s32[8]{0:T(128)S(1)} %get-tuple-element.91.n_ref, f32[8,128]{1,0:T(8,128)S(1)} %get-tuple-element.92.so_ref, ...), custom_call_target="tpu_custom_call" | custom-call | flops 9059696640 | bytes 31457280 | tf_op jit(solution)/shard_map/cond/branch_1_fun/pallas_call | solution.py:676
  185.3 0.3 copy.25
  185.7 0.9 reshape.34
  186.6 0.6 reshape.35
  187.2 13.3 %shard_map.137 = (bf16[169,128,128]{2,1,0:T(8,128)(2,1)}, f32[8,128]{1,0:T(8,128)}, f32[2,512,2304]{2,1,0:T(8,128)}) custom-call(f32[4,128]{1,0:T(4,128)} %pad_maximum_fusion.s_ref, bf16[512,512]{1,0:T(8,128)(2,1)} %constant.27.clone.perm_ref, bf16[8,2,16,2304]{3,2,1,0:T(8,128)(2,1)S(1)} %get-tuple-element.150.gf_ref, ...), custom_call_target="tpu_custom_call" | custom-call | flops 1073741824 | bytes 31457280 | tf_op jit(solution)/shard_map/pallas_call | solution.py:1022
  200.6 0.0 copy-start
  200.6 0.7 copy-done
  201.2 6.5 %shard_map.138 = f32[8,128]{1,0:T(8,128)S(1)} custom-call(f32[8,128]{1,0:T(8,128)S(1)} %copy-done), custom_call_target="tpu_custom_call" | custom-call | tf_op jit(solution)/shard_map/pallas_call | solution.py:1047
  207.7 0.1 reshape_squeeze.7
  207.9 0.2 slice_reduce_fusion.2
  208.1 0.1 reshape_squeeze.6
  208.2 0.2 slice_reduce_fusion.3
  208.4 0.6 pad_maximum_fusion.1
  209.0 0.6 copy.62
  (6 shorter events, 0.1 us)
Async XLA Ops:
  0.6 21.9 %copy-start.1 = (f32[2,4096]{1,0:T(2,128)S(1)}, f32[2,4096]{1,0:T(2,128)}, u32[]{:S(2)}) copy-start(f32[2,4096]{1,0:T(2,128)} %param.18) | copy-start | bytes 98308
  200.6 0.7 copy-start
